TPU v7x, 256 devices: a whole 4x4x8 slice. The times are simulated.
256 devices in a mesh: blk: 64 (over y, z, core), hd: 4 (over x).
Axes of the slice: x: 4, y: 4, z: 8, core: 2. Of those that a mesh axis runs over, the one named last changes fastest.
Arguments:
- queries: bfloat16 [1024, 256, 128], P('blk', 'hd'), may hold values from -10 to 10
- keys: bfloat16 [1024, 256, 128], P('blk', 'hd'), may hold values from -10 to 10
- values: bfloat16 [1024, 256, 128], P('blk', 'hd'), may hold values from -6 to 6
- out_weight: bfloat16 [256, 256], P('hd'), may hold values from -0.375 to 0.375
- out_grad: bfloat16 [1024, 128, 256], P('blk'), may hold values from -6 to 6
- pair_list: int32 [2, 2048], replicated, may hold values from 0 to 1023, as said below
Outputs:
- out: bfloat16 [1024, 128, 256], P('blk', 'hd')
- grad_q: bfloat16 [1024, 256, 128], P('blk', 'hd')
- grad_k: bfloat16 [1024, 256, 128], P('blk', 'hd')
- grad_v: bfloat16 [1024, 256, 128], P('blk', 'hd')
Inputs may be any that keep to these rules, and one draw needn't show every extreme that they name: `pair_list`: row 0 holds each pair's first block and row 1 its second. Pairs k * 32 to (k + 1) * 32 - 1 have their first block among blocks k * 16 to (k + 1) * 16 - 1; of these pairs at most 2 have their second block in any one range j * 16 to (j + 1) * 16 - 1, and exactly 2 for some range.
All inputs are finite; a program needn't handle non-finite values.
Results may differ from a plain program's by a relative error of at most 0.015.
Values may be sent and summed in bfloat16 or wider, within the bound.
A program may use at most 128 MiB of HBM per device.

v0:
```python
import math

import jax
import jax.numpy as jnp
from jax import lax
from jax.sharding import PartitionSpec as P

HEAD = 32


def lowered(tensor):
    return lax.optimization_barrier(tensor.astype(jnp.bfloat16)).astype(jnp.float32)


def pick_rows(source, index):
    padded = jnp.concatenate([source, jnp.zeros_like(source[:1])], axis=0)
    return jnp.take(padded, index, axis=0)


def by_groups(function, arrays):
    tile_count = arrays[0].shape[0]
    group_size = math.gcd(tile_count, 16)
    shaped = tuple(
        (item.reshape((tile_count // group_size, group_size) + item.shape[1:]) for item in arrays)
    )
    result = lax.map(lambda pieces: function(*pieces), shaped)
    return jax.tree.map(lambda item: item.reshape((tile_count,) + item.shape[2:]), result)


def tile_forward(q_tile, k_tile, v_tile):
    tile_count, feature_count, block_rows = q_tile.shape
    head_count = feature_count // HEAD
    four_shape = (tile_count, head_count, HEAD, block_rows)
    q_four = q_tile.reshape(four_shape)
    k_four = k_tile.reshape(four_shape)
    v_four = v_tile.reshape(four_shape)
    scores = jnp.einsum(
        "nher,nhec->nhrc", q_four, k_four, preferred_element_type=jnp.float32
    ) * HEAD ** (-0.5)
    row_top = jnp.max(scores, axis=3, keepdims=True)
    expo_scores = jnp.exp(scores - row_top)
    row_total = jnp.sum(expo_scores, axis=3, keepdims=True)
    tile_lse = (row_top + jnp.log(row_total))[..., 0]
    weights = (expo_scores / row_total).astype(jnp.bfloat16)
    tile_part = jnp.einsum("nhrc,nhec->nher", weights, v_four, preferred_element_type=jnp.float32)
    return (tile_part.reshape(tile_count, feature_count, block_rows), tile_lse)


def tile_backward(q_tile, k_tile, v_tile, grad_tile, lse_tile, delta_tile):
    tile_count, feature_count, block_rows = q_tile.shape
    head_count = feature_count // HEAD
    four_shape = (tile_count, head_count, HEAD, block_rows)
    q_four = q_tile.reshape(four_shape)
    k_four = k_tile.reshape(four_shape)
    v_four = v_tile.reshape(four_shape)
    g_four = grad_tile.reshape(four_shape)
    score_scale = HEAD ** (-0.5)
    scores = (
        jnp.einsum("nher,nhec->nhrc", q_four, k_four, preferred_element_type=jnp.float32)
        * score_scale
    )
    prob = jnp.exp(scores - lse_tile[..., None])
    prob_low = prob.astype(jnp.bfloat16)
    prob_grad = jnp.einsum("nher,nhec->nhrc", g_four, v_four, preferred_element_type=jnp.float32)
    score_grad = (prob * (prob_grad - delta_tile[..., None])).astype(jnp.bfloat16)
    term_q = (
        jnp.einsum("nhrc,nhec->nher", score_grad, k_four, preferred_element_type=jnp.float32)
        * score_scale
    )
    term_k = (
        jnp.einsum("nhrc,nher->nhec", score_grad, q_four, preferred_element_type=jnp.float32)
        * score_scale
    )
    term_v = jnp.einsum("nhrc,nher->nhec", prob_low, g_four, preferred_element_type=jnp.float32)
    out_shape = (tile_count, feature_count, block_rows)
    return (term_q.reshape(out_shape), term_k.reshape(out_shape), term_v.reshape(out_shape))


def merge_parts(part_out, part_lse, seg_ids, blk_dev, heads_here, block_rows):
    seg_top = jax.ops.segment_max(part_lse, seg_ids, num_segments=blk_dev + 1)
    seg_total = jax.ops.segment_sum(
        jnp.exp(part_lse - seg_top[seg_ids]), seg_ids, num_segments=blk_dev + 1
    )
    block_lse = seg_top + jnp.log(seg_total)
    part_weight = jnp.exp(part_lse - block_lse[seg_ids])
    scaled = part_out.reshape(-1, heads_here, HEAD, block_rows) * part_weight[:, :, None, :]
    attention = jax.ops.segment_sum(scaled, seg_ids, num_segments=blk_dev + 1)[:blk_dev]
    return (attention, block_lse[:blk_dev])


def local(queries, keys, values, out_weight, out_grad, pair_list):
    blk_dev, features_here, block_rows = queries.shape
    heads_here = features_here // HEAD
    owner_count = lax.axis_size("blk")
    own_index = lax.axis_index("blk")
    pair_dev = pair_list.shape[1] // owner_count
    capacity = max(2, (5 * pair_dev + 4 * owner_count - 1) // (4 * owner_count))
    slots_all = owner_count * capacity
    first_blocks = pair_list[0]
    second_blocks = pair_list[1]
    peer_owner = second_blocks // blk_dev
    grouped = peer_owner.reshape(owner_count, pair_dev)
    positions = jnp.arange(pair_dev, dtype=jnp.int32)
    before = positions[None, :] < positions[:, None]
    same_peer = grouped[:, :, None] == grouped[:, None, :]
    slot_rank = jnp.sum(same_peer & before[None], axis=2).reshape(-1)
    owners = jnp.arange(first_blocks.shape[0], dtype=jnp.int32) // pair_dev
    is_mine = peer_owner == own_index
    target = jnp.where(is_mine, owners * capacity + slot_rank, slots_all)
    marked = jax.ops.segment_sum(
        jnp.where(is_mine, second_blocks - own_index * blk_dev + 1, 0),
        target,
        num_segments=slots_all + 1,
    )[:slots_all]
    row_block = jnp.where(marked > 0, marked - 1, blk_dev)
    pair_start = own_index * pair_dev
    my_first = lax.dynamic_slice_in_dim(first_blocks, pair_start, pair_dev) - own_index * blk_dev
    my_peer = lax.dynamic_slice_in_dim(peer_owner, pair_start, pair_dev)
    my_slot = lax.dynamic_slice_in_dim(slot_rank, pair_start, pair_dev)
    dest_rows = my_peer * capacity + my_slot
    near_q = queries[my_first]
    near_k = keys[my_first]
    near_v = values[my_first]

    def placed(terms):
        return (
            jnp.zeros((slots_all,) + terms.shape[1:], jnp.bfloat16)
            .at[dest_rows]
            .set(terms.astype(jnp.bfloat16))
        )

    def home_sum(terms):
        return jax.ops.segment_sum(terms.astype(jnp.float32), row_block, num_segments=blk_dev + 1)[
            :blk_dev
        ]

    def local_sum(terms):
        return jax.ops.segment_sum(terms, my_first, num_segments=blk_dev)

    self_out, self_lse = by_groups(tile_forward, (queries, keys, values))
    seg_ids = jnp.concatenate([jnp.arange(blk_dev, dtype=jnp.int32), my_first, row_block])
    fetched_q, fetched_k, fetched_v = (
        lax.all_to_all(
            pick_rows(queries, row_block), "blk", split_axis=0, concat_axis=0, tiled=True
        ),
        lax.all_to_all(pick_rows(keys, row_block), "blk", split_axis=0, concat_axis=0, tiled=True),
        lax.all_to_all(
            pick_rows(values, row_block), "blk", split_axis=0, concat_axis=0, tiled=True
        ),
    )
    other_q = fetched_q[dest_rows]
    other_k = fetched_k[dest_rows]
    other_v = fetched_v[dest_rows]
    fwd_out, fwd_lse = by_groups(tile_forward, (near_q, other_k, other_v))
    rev_out, rev_lse = by_groups(tile_forward, (other_q, near_k, near_v))
    back_out = (
        jnp.zeros((slots_all, features_here, block_rows), jnp.float32).at[dest_rows].set(rev_out)
    )
    back_lse = (
        jnp.zeros((slots_all, heads_here, block_rows), jnp.float32).at[dest_rows].set(rev_lse)
    )
    got_out, got_lse = (
        lax.all_to_all(back_out, "blk", split_axis=0, concat_axis=0, tiled=True),
        lax.all_to_all(back_lse, "blk", split_axis=0, concat_axis=0, tiled=True),
    )
    part_out = jnp.concatenate([self_out, fwd_out, got_out], axis=0)
    part_lse = jnp.concatenate([self_lse, fwd_lse, got_lse], axis=0)
    attention, lse_own = merge_parts(part_out, part_lse, seg_ids, blk_dev, heads_here, block_rows)
    attn_low = attention.astype(jnp.bfloat16).reshape(blk_dev, features_here, block_rows)
    partial_out = jnp.einsum(
        "bfr,fo->bro", attn_low, out_weight, preferred_element_type=jnp.float32
    )
    out = lax.psum_scatter(partial_out.astype(jnp.bfloat16), "hd", scatter_dimension=1, tiled=True)
    attn_grad = jnp.einsum(
        "bro,fo->bfr", out_grad, out_weight, preferred_element_type=jnp.float32
    ).astype(jnp.bfloat16)
    row_delta = jnp.sum(
        attn_grad.astype(jnp.float32).reshape(blk_dev, heads_here, HEAD, block_rows) * attention,
        axis=2,
    )
    self_q, self_k, self_v = by_groups(
        tile_backward, (queries, keys, values, attn_grad, lse_own, row_delta)
    )
    fwd_q, fwd_k, fwd_v = by_groups(
        tile_backward,
        (near_q, other_k, other_v, attn_grad[my_first], lse_own[my_first], row_delta[my_first]),
    )
    sent_grad = lax.all_to_all(
        pick_rows(attn_grad, row_block), "blk", split_axis=0, concat_axis=0, tiled=True
    )
    sent_lse, sent_delta = (
        lax.all_to_all(
            pick_rows(lse_own, row_block), "blk", split_axis=0, concat_axis=0, tiled=True
        ),
        lax.all_to_all(
            pick_rows(row_delta, row_block), "blk", split_axis=0, concat_axis=0, tiled=True
        ),
    )
    other_grad = sent_grad[dest_rows]
    other_lse = sent_lse[dest_rows]
    other_delta = sent_delta[dest_rows]
    rev_q, rev_k, rev_v = by_groups(
        tile_backward, (other_q, near_k, near_v, other_grad, other_lse, other_delta)
    )
    got_q, got_k, got_v = (
        lax.all_to_all(placed(rev_q), "blk", split_axis=0, concat_axis=0, tiled=True),
        lax.all_to_all(placed(fwd_k), "blk", split_axis=0, concat_axis=0, tiled=True),
        lax.all_to_all(placed(fwd_v), "blk", split_axis=0, concat_axis=0, tiled=True),
    )
    grad_q = self_q + local_sum(fwd_q) + home_sum(got_q)
    grad_k = self_k + local_sum(lowered(rev_k)) + home_sum(got_k)
    grad_v = self_v + local_sum(lowered(rev_v)) + home_sum(got_v)
    return (
        out,
        grad_q.astype(jnp.bfloat16),
        grad_k.astype(jnp.bfloat16),
        grad_v.astype(jnp.bfloat16),
    )


def solution(mesh):
    return jax.shard_map(
        local,
        mesh=mesh,
        in_specs=(
            P("blk", "hd", None),
            P("blk", "hd", None),
            P("blk", "hd", None),
            P("hd", None),
            P("blk", None, None),
            P(),
        ),
        out_specs=(
            P("blk", "hd", None),
            P("blk", "hd", None),
            P("blk", "hd", None),
            P("blk", "hd", None),
        ),
        check_vma=False,
    )
```

profile of v0, /device:TPU:1, one launch (start us, length us, event | category | flops | bytes accessed | tf_op | source)
XLA Modules:
  0.0 668.7 jit_solution(13962634877053969480)
XLA Ops:
  9.5 14.7 %scatter_custom_fusion = s32[129]{0:T(256)S(1)} fusion(s32[2048]{0:T(1024)S(1)} %bitcast.310, s32[2048]{0:T(1024)S(1)} %get-tuple-element.337, s32[]{:T(128)} %copy.113), kind=kCustom, calls=%fused_computation.168 | custom fusion | flops 2048 | bytes 520 | tf_op jit(solution)/shard_map/scatter-add | solution.py:110
  39.5 64.3 %all_to_all.55 = bf16[128,64,128]{2,1,0:T(8,128)(2,1)} all-to-all(bf16[128,64,128]{2,1,0:T(8,128)(2,1)S(1)} %get-tuple-element.343), channel_id=1, replica_groups=mesh['blk'=64,'hd'=4] {'blk'}, dimensions={0} | all-to-all | bytes 4194304 | tf_op jit(solution)/shard_map/all_to_all | solution.py:147
  103.8 57.0 %all_to_all.56 = bf16[128,64,128]{2,1,0:T(8,128)(2,1)} all-to-all(bf16[128,64,128]{2,1,0:T(8,128)(2,1)S(1)} %get-tuple-element.342), channel_id=1, replica_groups=mesh['blk'=64,'hd'=4] {'blk'}, dimensions={0} | all-to-all | bytes 4194304 | tf_op jit(solution)/shard_map/all_to_all | solution.py:143
  160.7 6.0 all-to-all-start.1
  181.0 36.8 %all-to-all-done.1 = bf16[128,64,128]{2,1,0:T(8,128)(2,1)} async-done(((bf16[128,64,128]{2,1,0:T(8,128)(2,1)}), bf16[128,64,128]{2,1,0:T(8,128)(2,1)}, u32[]{:S(2)}, u32[]{:S(2)}) %all-to-all-start.1) | async-done | bytes 2097184 | tf_op jit(solution)/shard_map/all_to_all | solution.py:146
  234.7 7.9 %all-to-all-start.3 = ((f32[128,64,128]{2,1,0:T(8,128)}), f32[128,64,128]{2,1,0:T(8,128)}, u32[]{:S(2)}, u32[]{:S(2)}) async-start(f32[128,64,128]{2,1,0:T(8,128)} %scatter_fusion), calls=%async_computation.3 | async-start | bytes 8388608 | tf_op jit(solution)/shard_map/all_to_all | solution.py:163
  250.9 87.6 %all-to-all-done.3 = f32[128,64,128]{2,1,0:T(8,128)} async-done(((f32[128,64,128]{2,1,0:T(8,128)}), f32[128,64,128]{2,1,0:T(8,128)}, u32[]{:S(2)}, u32[]{:S(2)}) %all-to-all-start.3) | async-done | bytes 4194336 | tf_op jit(solution)/shard_map/all_to_all | solution.py:163
  345.6 6.8 %while.19 = (s32[]{:T(128)}, f32[2,16,64,128]{3,2,1,0:T(8,128)}, f32[2,16,2,128]{3,2,1,0:T(2,128)S(1)}, bf16[2,16,64,128]{3,2,1,0:T(8,128)(2,1)S(1)}, bf16[2,16,...) while((s32[]{:T(128)}, f32[2,16,64,128]{3,2,1,0:T(8,128)}, ...), condition=%wide.region_7.9_spmd, body=%wide.region_4.8_spmd.sunk | while | flops 71823360 | bytes 10355289 | solution.py:26
  354.3 11.9 %scatter_fusion.2 = f32[17,2,128]{2,1,0:T(2,128)S(1)} fusion(f32[17,2,128]{2,1,0:T(2,128)S(1)} %broadcast_in_dim.147, s32[176]{0:T(256)S(1)} %pad_add_fusion, f32[176,2,128]{2,1,0:T(2,128)} %pad_maximum_fusion), kind=kCustom, calls=%fused_computation.23 | custom fusion | flops 45056 | bytes 541376 | tf_op jit(solution)/shard_map/scatter-max | solution.py:80
  369.5 11.9 %scatter_fusion.3 = f32[17,2,128]{2,1,0:T(2,128)S(1)} fusion(f32[17,2,128]{2,1,0:T(2,128)S(1)} %broadcast_in_dim.148, s32[176]{0:T(256)S(1)} %pad_add_fusion, f32[176,2,128]{2,1,0:T(2,128)} %subtract_exponential_fusion.7), kind=kCustom, calls=%fused_computation.24 | custom fusion | flops 45056 | bytes 541376 | tf_op jit(solution)/shard_map/scatter-add | solution.py:81
  385.9 6.5 maximum_multiply_fusion
  392.5 18.4 %scatter_fusion.4 = f32[17,2,32,128]{3,2,1,0:T(8,128)S(1)} fusion(f32[17,2,32,128]{3,2,1,0:T(8,128)S(1)} %broadcast_in_dim.139, s32[176]{0:T(256)S(1)} %copy-done.32, f32[176,2,32,128]{3,2,1,0:T(8,128)} %maximum_multiply_fusion), kind=kCustom, calls=%fused_computation.25 | custom fusion | flops 1441792 | bytes 17302208 | tf_op jit(solution)/shard_map/scatter-add | solution.py:87
  412.9 10.6 %all-to-all-start.7 = ((f32[128,2,128]{2,1,0:T(2,128)}), f32[128,2,128]{2,1,0:T(2,128)}, u32[]{:S(2)}, u32[]{:S(2)}) async-start(f32[128,2,128]{2,1,0:T(2,128)} %get-tuple-element.338), calls=%async_computation.8 | async-start | bytes 262144 | tf_op jit(solution)/shard_map/all_to_all | solution.py:195
  433.8 6.0 all-to-all-start.5
  440.9 14.3 %while.66 = (s32[]{:T(128)}, f32[2,16,64,128]{3,2,1,0:T(8,128)}, bf16[2,16,64,128]{3,2,1,0:T(8,128)(2,1)}, bf16[2,16,64,128]{3,2,1,0:T(8,128)(2,1)}, bf16[2,16,6...) while((s32[]{:T(128)}, f32[2,16,64,128]{3,2,1,0:T(8,128)}, ...), condition=%wide.region_24.27_spmd, body=%wide.region_23.26_spmd.sunk | while | flops 172359680 | bytes 29345032 | solution.py:26
  461.8 10.5 %all-to-all-start.10 = ((bf16[128,64,128]{2,1,0:T(8,128)(2,1)}), bf16[128,64,128]{2,1,0:T(8,128)(2,1)}, u32[]{:S(2)}, u32[]{:S(2)}) async-start(bf16[128,64,128]{2,1,0:T(8,128)(2,1)} %scatter_fusion.11), calls=%async_computation.11 | async-start | bytes 4194304 | tf_op jit(solution)/shard_map/all_to_all | solution.py:208
  487.6 35.8 %all-to-all-done.10 = bf16[128,64,128]{2,1,0:T(8,128)(2,1)} async-done(((bf16[128,64,128]{2,1,0:T(8,128)(2,1)}), bf16[128,64,128]{2,1,0:T(8,128)(2,1)}, u32[]{:S(2)}, u32[]{:S(2)}) %all-to-all-start.10) | async-done | bytes 2097184 | tf_op jit(solution)/shard_map/all_to_all | solution.py:208
  523.5 6.0 all-to-all-start.9
  529.5 12.9 %while.21 = (s32[]{:T(128)}, bf16[2,16,64,128]{3,2,1,0:T(8,128)(2,1)S(1)}, bf16[2,16,64,128]{3,2,1,0:T(8,128)(2,1)}, bf16[2,16,64,128]{3,2,1,0:T(8,128)(2,1)}, b...) while((s32[]{:T(128)}, ...), condition=%wide.region_20.23_spmd, body=%wide.region_19.22_spmd.sunk | while | flops 172490752 | bytes 24363788 | solution.py:26
  548.6 32.0 %all-to-all-done.9 = bf16[128,64,128]{2,1,0:T(8,128)(2,1)} async-done(((bf16[128,64,128]{2,1,0:T(8,128)(2,1)}), bf16[128,64,128]{2,1,0:T(8,128)(2,1)}, u32[]{:S(2)}, u32[]{:S(2)}) %all-to-all-start.9) | async-done | bytes 2097184 | tf_op jit(solution)/shard_map/all_to_all | solution.py:207
  580.6 6.0 all-to-all-start.8
  599.2 13.6 %scatter_fusion.12 = f32[17,64,128]{2,1,0:T(8,128)S(1)} fusion(f32[17,64,128]{2,1,0:T(8,128)S(1)} %broadcast.347.clone.2, s32[128]{0:T(128)S(1)} %copy-done.34, f32[128,64,128]{2,1,0:T(8,128)} %convert_element_type.121), kind=kCustom, calls=%fused_computation.33 | custom fusion | flops 1048576 | bytes 12583424 | tf_op jit(solution)/shard_map/scatter-add | solution.py:133
  622.6 13.6 %scatter_fusion.9 = f32[17,64,128]{2,1,0:T(8,128)S(1)} fusion(f32[17,64,128]{2,1,0:T(8,128)S(1)} %broadcast.347.clone.1, s32[128]{0:T(128)S(1)} %copy-done.34, f32[128,64,128]{2,1,0:T(8,128)} %convert_element_type.113), kind=kCustom, calls=%fused_computation.30 | custom fusion | flops 1048576 | bytes 12583424 | tf_op jit(solution)/shard_map/scatter-add | solution.py:133
  643.2 13.6 %scatter_fusion.6 = f32[17,64,128]{2,1,0:T(8,128)S(1)} fusion(f32[17,64,128]{2,1,0:T(8,128)S(1)} %broadcast.347.clone, s32[128]{0:T(128)S(1)} %copy-done.34, f32[128,64,128]{2,1,0:T(8,128)} %convert_element_type.109), kind=kCustom, calls=%fused_computation.27 | custom fusion | flops 1048576 | bytes 12583424 | tf_op jit(solution)/shard_map/scatter-add | solution.py:133
  (294 shorter events, 187.3 us)
Async XLA Ops:
  24.2 219.2 %copy-start.33 = (s32[128]{0:T(128)}, s32[128]{0:T(128)S(1)}, u32[]{:S(2)}) copy-start(s32[128]{0:T(128)S(1)} %get-tuple-element.305) | copy-start | bytes 1540
  160.7 57.2 %all-to-all-start.1 = ((bf16[128,64,128]{2,1,0:T(8,128)(2,1)}), bf16[128,64,128]{2,1,0:T(8,128)(2,1)}, u32[]{:S(2)}, u32[]{:S(2)}) async-start(bf16[128,64,128]{2,1,0:T(8,128)(2,1)} %get-tuple-element.341), calls=%async_computation.1 | async-start | bytes 4194304 | tf_op jit(solution)/shard_map/all_to_all | solution.py:146
  166.9 76.5 %copy-start.29 = (s32[1,32]{1,0:T(1,128)}, s32[1,32]{1,0:T(1,128)S(1)}, u32[]{:S(2)}) copy-start(s32[1,32]{1,0:T(1,128)S(1)} %get-tuple-element.307) | copy-start | bytes 388
  166.9 75.7 %copy-start.37 = (s32[1024]{0:T(1024)}, s32[1024]{0:T(1024)S(1)}, u32[]{:S(2)}) copy-start(s32[1024]{0:T(1024)S(1)} %pad_clamp_fusion.1) | copy-start | bytes 12292
  168.3 79.6 %copy-start.35 = (s32[1024]{0:T(1024)}, s32[1024]{0:T(1024)S(1)}, u32[]{:S(2)}) copy-start(s32[1024]{0:T(1024)S(1)} %pad_clamp_fusion.2) | copy-start | bytes 12292
  176.6 49.6 %copy-start.2 = (bf16[2,16,64,128]{3,2,1,0:T(8,128)(2,1)}, bf16[2,16,64,128]{3,2,1,0:T(8,128)(2,1)S(1)}, u32[]{:S(2)}) copy-start(bf16[2,16,64,128]{3,2,1,0:T(8,128)(2,1)S(1)} %get-tuple-element.693) | copy-start | bytes 1572868
  176.6 49.6 %copy-start.6 = (bf16[2,16,64,128]{3,2,1,0:T(8,128)(2,1)}, bf16[2,16,64,128]{3,2,1,0:T(8,128)(2,1)S(1)}, u32[]{:S(2)}) copy-start(bf16[2,16,64,128]{3,2,1,0:T(8,128)(2,1)S(1)} %get-tuple-element.695) | copy-start | bytes 1572868
  176.6 49.6 %copy-start.7 = (bf16[2,16,64,128]{3,2,1,0:T(8,128)(2,1)}, bf16[2,16,64,128]{3,2,1,0:T(8,128)(2,1)S(1)}, u32[]{:S(2)}) copy-start(bf16[2,16,64,128]{3,2,1,0:T(8,128)(2,1)S(1)} %get-tuple-element.696) | copy-start | bytes 1572868
  217.9 16.2 %all-to-all-start.4 = ((f32[128,2,128]{2,1,0:T(2,128)}), f32[128,2,128]{2,1,0:T(2,128)S(1)}, u32[]{:S(2)}, u32[]{:S(2)}) async-start(f32[128,2,128]{2,1,0:T(2,128)} %scatter_fusion.1), calls=%async_computation.4 | async-start | bytes 262144 | tf_op jit(solution)/shard_map/all_to_all | solution.py:164
  234.7 103.8 %all-to-all-start.3 = ((f32[128,64,128]{2,1,0:T(8,128)}), f32[128,64,128]{2,1,0:T(8,128)}, u32[]{:S(2)}, u32[]{:S(2)}) async-start(f32[128,64,128]{2,1,0:T(8,128)} %scatter_fusion), calls=%async_computation.3 | async-start | bytes 8388608 | tf_op jit(solution)/shard_map/all_to_all | solution.py:163
  243.4 126.2 %copy-start.31 = (s32[176]{0:T(256)}, s32[176]{0:T(256)S(1)}, u32[]{:S(2)}) copy-start(s32[176]{0:T(256)S(1)} %pad_add_fusion) | copy-start | bytes 2116
  243.5 122.7 %copy-start.38 = (s32[1024]{0:T(1024)}, s32[1024]{0:T(1024)S(1)}, u32[]{:S(2)}) copy-start(s32[1024]{0:T(1024)S(1)} %pad_clamp_fusion) | copy-start | bytes 12292
  338.5 74.4 %all-to-all-start.6 = ((bf16[128,64,128]{2,1,0:T(8,128)(2,1)}), bf16[128,64,128]{2,1,0:T(8,128)(2,1)}, u32[]{:S(2)}, u32[]{:S(2)}) async-start(bf16[128,64,128]{2,1,0:T(8,128)(2,1)} %get-tuple-element.340), calls=%async_computation.7 | async-start | bytes 4194304 | tf_op jit(solution)/shard_map/all_to_all | solution.py:188
  352.4 33.5 %copy-start.4 = (bf16[2,16,64,128]{3,2,1,0:T(8,128)(2,1)}, bf16[2,16,64,128]{3,2,1,0:T(8,128)(2,1)S(1)}, u32[]{:S(2)}) copy-start(bf16[2,16,64,128]{3,2,1,0:T(8,128)(2,1)S(1)} %get-tuple-element.694) | copy-start | bytes 1572868
  352.4 33.5 %copy-start.8 = (bf16[2,16,64,128]{3,2,1,0:T(8,128)(2,1)}, bf16[2,16,64,128]{3,2,1,0:T(8,128)(2,1)S(1)}, u32[]{:S(2)}) copy-start(bf16[2,16,64,128]{3,2,1,0:T(8,128)(2,1)S(1)} %get-tuple-element.697) | copy-start | bytes 1572868
  352.4 29.0 %copy-start.41 = (pred[17]{0:T(512)(128)(4,1)S(1)}, pred[17]{0:T(512)(128)(4,1)}, u32[]{:S(2)}) copy-start(pred[17]{0:T(512)(128)(4,1)} %constant.202.clone.1) | copy-start | bytes 55
  392.5 19.5 %copy-start.25 = (f32[128,2,128]{2,1,0:T(2,128)S(1)}, f32[128,2,128]{2,1,0:T(2,128)}, u32[]{:S(2)}) copy-start(f32[128,2,128]{2,1,0:T(2,128)} %gather_fusion.17) | copy-start | bytes 393220
  412.9 20.8 %all-to-all-start.7 = ((f32[128,2,128]{2,1,0:T(2,128)}), f32[128,2,128]{2,1,0:T(2,128)}, u32[]{:S(2)}, u32[]{:S(2)}) async-start(f32[128,2,128]{2,1,0:T(2,128)} %get-tuple-element.338), calls=%async_computation.8 | async-start | bytes 262144 | tf_op jit(solution)/shard_map/all_to_all | solution.py:195
  433.8 28.0 %all-to-all-start.5 = ((f32[128,2,128]{2,1,0:T(2,128)}), f32[128,2,128]{2,1,0:T(2,128)}, u32[]{:S(2)}, u32[]{:S(2)}) async-start(f32[128,2,128]{2,1,0:T(2,128)} %get-tuple-element.339), calls=%async_computation.6 | async-start | bytes 262144 | tf_op jit(solution)/shard_map/all_to_all | solution.py:192
  461.8 61.7 %all-to-all-start.10 = ((bf16[128,64,128]{2,1,0:T(8,128)(2,1)}), bf16[128,64,128]{2,1,0:T(8,128)(2,1)}, u32[]{:S(2)}, u32[]{:S(2)}) async-start(bf16[128,64,128]{2,1,0:T(8,128)(2,1)} %scatter_fusion.11), calls=%async_computation.11 | async-start | bytes 4194304 | tf_op jit(solution)/shard_map/all_to_all | solution.py:208
  523.5 57.2 %all-to-all-start.9 = ((bf16[128,64,128]{2,1,0:T(8,128)(2,1)}), bf16[128,64,128]{2,1,0:T(8,128)(2,1)}, u32[]{:S(2)}, u32[]{:S(2)}) async-start(bf16[128,64,128]{2,1,0:T(8,128)(2,1)} %scatter_fusion.8), calls=%async_computation.10 | async-start | bytes 4194304 | tf_op jit(solution)/shard_map/all_to_all | solution.py:207
  548.6 38.4 %copy-start.28 = (bf16[64,256]{1,0:T(8,128)(2,1)S(1)}, bf16[64,256]{1,0:T(8,128)(2,1)}, u32[]{:S(2)}) copy-start(bf16[64,256]{1,0:T(8,128)(2,1)} %param.21) | copy-start | bytes 98308
  580.6 58.5 %all-to-all-start.8 = ((bf16[128,64,128]{2,1,0:T(8,128)(2,1)}), bf16[128,64,128]{2,1,0:T(8,128)(2,1)}, u32[]{:S(2)}, u32[]{:S(2)}) async-start(bf16[128,64,128]{2,1,0:T(8,128)(2,1)} %scatter_fusion.5), calls=%async_computation.9 | async-start | bytes 4194304 | tf_op jit(solution)/shard_map/all_to_all | solution.py:206
  586.6 74.8 %reduce-scatter.2.cloned.1.call-start = ((), (), s32[]{:S(2)}) async-start(), calls=%async_computation.12 | async-start | bytes 1310720 | tf_op jit(solution)/shard_map/reduce_scatter | solution.py:173
  (38 other events, 146.1 us)
Sparse Core Ops, SparseCore 0:
  590.6 25.6 reduce-scatter.1
where the time goes:
time: 682 us; the launch traced here: 669 us
  waiting for transfers between devices  200 us (29%)
  other arithmetic  147 us (22%)
  blocking collectives  121 us (18%)
  local copies, waits for them, and re-layouts  91.3 us (13%)
  starting transfers between devices  65 us (10%)
  matrix products  28.9 us (4%)
  between operations  15.2 us (2%)
    all_to_all x1, waiting for transfers between devices, local(): lax.all_to_all(back_out, 'blk', split_axis=0, concat_axis=0, tiled=True)  87.6 us
    all_to_all x1, blocking collectives, local(): lax.all_to_all(pick_rows(values, row_block), 'blk', split_axis=0, concat_...  64.3 us
    all_to_all x1, blocking collectives, local(): lax.all_to_all(pick_rows(queries, row_block), 'blk', split_axis=0, concat...  57 us
    scatter-add x3, other arithmetic, home_sum(): jax.ops.segment_sum(terms.astype(jnp.float32), row_block, num_segments=bl...  40.8 us
    all_to_all x1, waiting for transfers between devices, local(): lax.all_to_all(pick_rows(keys, row_block), 'blk', split_axis=0, concat_ax...  36.8 us
    all_to_all x1, waiting for transfers between devices, local(): lax.all_to_all(placed(fwd_v), 'blk', split_axis=0, concat_axis=0, tiled=T...  35.8 us
    all_to_all x1, waiting for transfers between devices, local(): lax.all_to_all(placed(fwd_k), 'blk', split_axis=0, concat_axis=0, tiled=T...  32 us
    scatter-add x1, other arithmetic, merge_parts(): jax.ops.segment_sum(scaled, seg_ids, num_segments=blk_dev + 1)[:blk_dev]  18.4 us
  transfers between devices with their start and end apart: 10, of which 6 were waited for; matrix products, arithmetic and copies ran while one was open for 35% of the time, Pallas kernels for 0%

commit v1 on v0

v1 whole, which is shorter than its diff:
```python
import functools

import jax
import jax.numpy as jnp
from jax import lax
from jax.experimental import pallas as pl
from jax.experimental.pallas import tpu as pltpu
from jax.sharding import PartitionSpec as P

MESH = pl.DeviceIdType.MESH
HEAD = 32
NY, NZ, NX = 4, 8, 4
BLK = 16
PART_A = 10
PART_B = BLK - PART_A
BASE_B = 2 * NY * NZ * PART_A
SLOTS = 2 * NY * NZ * BLK
UNROLL = 4
LIST = 192
NEG = -1e30
RATE = HEAD**-0.5 * 1.4426950408889634
SCALE = HEAD**-0.5
F32 = jnp.float32
BF16 = jnp.bfloat16


def place():
    blk, hd = lax.axis_index("blk"), lax.axis_index("hd")
    core, z, y = blk % 2, (blk // 2) % NZ, blk // (2 * NZ)

    def device(yy, zz, cc, xx):
        return ((yy * NZ + zz) * 2 + cc, xx)

    return y, z, core, hd, device


def slot_of(block):
    dev, inner = block // BLK, block % BLK
    core, z, y = dev % 2, (dev // 2) % NZ, dev // (2 * NZ)
    in_a = ((core * NY + y) * NZ + z) * PART_A + inner
    in_b = BASE_B + ((core * NZ + z) * NY + y) * PART_B + inner - PART_A
    return jnp.where(inner < PART_A, in_a, in_b)


def meet(peers):
    barrier = pltpu.get_barrier_semaphore()
    for peer in peers:
        pl.semaphore_signal(barrier, inc=1, device_id=peer, device_id_type=MESH)
    pl.semaphore_wait(barrier, len(peers))


class Gather:
    SEMS = 48

    def __init__(self, buffer, send_sem, recv_sem, coords, base=0):
        self.buffer, self.send_sem, self.recv_sem = buffer, send_sem, recv_sem
        self.y, self.z, self.core, hd, device = coords
        y, z, core = self.y, self.z, self.core
        self.z_next, self.z_last = device(y, (z + 1) % NZ, core, hd), device(y, (z + NZ - 1) % NZ, core, hd)
        self.y_next, self.y_last = device((y + 1) % NY, z, core, hd), device((y + NY - 1) % NY, z, core, hd)
        self.twin = device(y, z, 1 - core, hd)
        self.base = base
        self.sent = []

    def peers(self):
        return [self.z_next, self.z_last, self.y_next, self.y_last, self.twin]

    def rows_a(self, core, y, z, start, count):
        return self.buffer.at[pl.ds(((core * NY + y) * NZ + z) * PART_A + start, count)]

    def rows_b(self, core, z, y, start, count):
        return self.buffer.at[pl.ds(BASE_B + ((core * NZ + z) * NY + y) * PART_B + start, count)]

    def own(self):
        return (
            self.rows_a(self.core, self.y, self.z, 0, PART_A),
            self.rows_b(self.core, self.z, self.y, 0, PART_B),
        )

    def copy(self, rows, peer, sem):
        sem += self.base
        return pltpu.make_async_remote_copy(
            src_ref=rows, dst_ref=rows, send_sem=self.send_sem.at[sem], recv_sem=self.recv_sem.at[sem],
            device_id=peer, device_id_type=MESH)

    def leg(self, kind, step, way, arriving):
        hop = step + 1 if arriving else step
        sign = -1 if way == 0 else 1
        zz, yy = (self.z + sign * hop + 2 * NZ) % NZ, (self.y + sign * hop + 2 * NY) % NY
        core = self.core
        if kind == "az":
            half = PART_A // 2
            rows = self.rows_a(core, self.y, zz, 0, PART_A) if step < 3 else self.rows_a(core, self.y, zz, way * half, half)
            sem = 0 + 2 * step + way
        elif kind == "by":
            half = PART_B // 2
            rows = self.rows_b(core, self.z, yy, 0, PART_B) if step < 1 else self.rows_b(core, self.z, yy, way * half, half)
            sem = 8 + 2 * step + way
        elif kind == "ay":
            rows = self.rows_a(core, yy, 0, 0, NZ * PART_A) if step < 1 else self.rows_a(core, yy, 4 * way, 0, 4 * PART_A)
            sem = 12 + 2 * step + way
        else:
            rows = self.rows_b(core, zz, 0, 0, NY * PART_B) if step < 3 else self.rows_b(core, zz, 2 * way, 0, 2 * PART_B)
            sem = 16 + 2 * step + way
        along_z = kind in ("az", "bz")
        peer = (self.z_next if way == 0 else self.z_last) if along_z else (self.y_next if way == 0 else self.y_last)
        return self.copy(rows, peer, sem)

    def send(self, kind, step):
        for way in (0, 1):
            leg = self.leg(kind, step, way, False)
            leg.start()
            self.sent.append(leg)

    def forward(self, kind, step):
        for way in (0, 1):
            self.leg(kind, step, way, True).wait_recv()
            leg = self.leg(kind, step + 1, way, False)
            leg.start()
            self.sent.append(leg)

    def arrive(self, kind, step):
        for way in (0, 1):
            self.leg(kind, step, way, True).wait_recv()

    def twin_a(self, hop, core):
        return self.copy(self.rows_a(core, (self.y + hop + NY) % NY, 0, 0, NZ * PART_A), self.twin, 24 + hop % NY)

    def twin_b(self, hop, core):
        return self.copy(self.rows_b(core, (self.z + hop + NZ) % NZ, 0, 0, NY * PART_B), self.twin, 28 + hop % NZ)

    def pass_on(self, which, *hops):
        for hop in hops:
            leg = which(hop, self.core)
            leg.start()
            self.sent.append(leg)

    def steps(self):
        return [
            lambda: (self.send("az", 0), self.send("by", 0)),
            lambda: self.forward("by", 0),
            lambda: self.forward("az", 0),
            lambda: (self.arrive("by", 1), self.send("bz", 0), self.pass_on(self.twin_b, 0)),
            lambda: self.forward("az", 1),
            lambda: self.forward("az", 2),
            lambda: (self.arrive("az", 3), self.send("ay", 0), self.pass_on(self.twin_a, 0)),
            lambda: (self.forward("bz", 0), self.pass_on(self.twin_b, -1, 1)),
            lambda: (self.forward("bz", 1), self.pass_on(self.twin_b, -2, 2)),
            lambda: (self.forward("ay", 0), self.pass_on(self.twin_a, -1, 1)),
            lambda: (self.forward("bz", 2), self.pass_on(self.twin_b, -3, 3)),
            lambda: (self.arrive("ay", 1), self.pass_on(self.twin_a, 2)),
            lambda: (self.arrive("bz", 3), self.pass_on(self.twin_b, 4)),
            self.finish,
        ]

    def finish(self):
        for hop in range(NY):
            self.twin_a(hop, 1 - self.core).wait_recv()
        for hop in range(NZ):
            self.twin_b(hop, 1 - self.core).wait_recv()
        for leg in self.sent:
            leg.wait_send()


def gather_kernel(k_ref, v_ref, q_ref, g_ref, kv_ref, qg_ref, local_sem, send_sem, recv_sem):
    coords = place()
    kv = Gather(kv_ref, send_sem, recv_sem, coords)
    qg = Gather(qg_ref, send_sem, recv_sem, coords, Gather.SEMS)
    copies = []
    for number, (gather, refs) in enumerate(((kv, (k_ref, v_ref)), (qg, (q_ref, g_ref)))):
        for side, ref in enumerate(refs):
            rows_a, rows_b = gather.own()
            features = pl.ds(64 * side, 64)
            copies.append(pltpu.make_async_copy(ref.at[pl.ds(0, PART_A)], rows_a.at[:, features], local_sem.at[4 * number + 2 * side]))
            copies.append(pltpu.make_async_copy(ref.at[pl.ds(PART_A, PART_B)], rows_b.at[:, features], local_sem.at[4 * number + 2 * side + 1]))
    for copy in copies:
        copy.start()
    meet(kv.peers())
    for copy in copies:
        copy.wait()
    for step in kv.steps()[:-1]:
        step()
    for step in qg.steps()[:-1]:
        step()
    kv.finish()
    qg.finish()


def gather_all(keys, values, queries, grads):
    shape = jax.ShapeDtypeStruct((SLOTS, 128, 128), BF16)
    sem = pltpu.SemaphoreType.DMA
    anywhere = pl.BlockSpec(memory_space=pl.ANY)
    return pl.pallas_call(
        gather_kernel, out_shape=(shape, shape), in_specs=[anywhere] * 4, out_specs=(anywhere,) * 2,
        scratch_shapes=[sem((8,)), sem((2 * Gather.SEMS,)), sem((2 * Gather.SEMS,))],
        compiler_params=pltpu.CompilerParams(collective_id=0, has_side_effects=True),
        name="gather_rows",
    )(keys, values, queries, grads)


def spread(first, second):
    parts = (first[:HEAD], first[HEAD:], second[:HEAD], second[HEAD:])
    zero = jnp.zeros((HEAD, 128), first.dtype)
    rows = [jnp.concatenate([part if col == row else zero for col in range(4)], axis=1) for row, part in enumerate(parts)]
    return jnp.concatenate(rows, axis=0)


def diagonal(full, top):
    return full[top:top + HEAD, :128], full[top + HEAD:top + 2 * HEAD, 128:]


def dot(a, b):
    return jnp.dot(a, b, preferred_element_type=F32)


def dot_nt(a, b):
    return lax.dot_general(a, b, (((1,), (1,)), ((), ())), preferred_element_type=F32)


def query_tile(kv, right):
    both = dot(kv.T, right)
    scores, prob_grad = both[:, :256], both[:, 256:]
    top = jnp.max(scores, axis=0, keepdims=True)
    expo = jnp.exp2((scores - top) * RATE)
    total = jnp.sum(expo, axis=0, keepdims=True)
    weighed = jnp.sum(expo * prob_grad, axis=0, keepdims=True)
    mean = weighed / total
    change = (expo * (prob_grad - mean)).astype(BF16)
    by_expo = dot(kv, expo.astype(BF16))
    by_change = dot(kv[:64], change)
    heads = []
    for h in range(2):
        cols = slice(128 * h, 128 * h + 128)
        b = diagonal(by_expo, 0)[h]
        o = diagonal(by_expo, 64)[h]
        a = diagonal(by_change, 0)[h] + mean[:, cols] * b
        heads.append((top[:, cols], total[:, cols], weighed[:, cols], o, a, b))
    return heads


def query_merge(old, new, reset, skip):
    merged = []
    for (m0, *acc), (m1, *add) in zip(old, new):
        m0, m1 = m0 + reset, m1 + skip
        m = jnp.maximum(m0, m1)
        w0, w1 = jnp.exp2((m0 - m) * RATE), jnp.exp2((m1 - m) * RATE)
        merged.append((m, *[x * w0 + y * w1 for x, y in zip(acc, add)]))
    return merged


def query_result(state):
    rows, grads, stats = [], [], []
    for m, total, weighed, o, a, b in state:
        inverse = 1.0 / total
        delta = weighed * inverse
        rows.append((o * inverse).astype(BF16))
        grads.append(((a - delta * b) * (inverse * SCALE)).astype(BF16))
        stats.append((m + jnp.log2(total) * (1.0 / RATE), delta))
    aux = [stats[0][0], stats[1][0], stats[0][1], stats[1][1], jnp.zeros((4, 128), F32)]
    return jnp.concatenate(rows, axis=0), jnp.concatenate(grads, axis=0), jnp.concatenate(aux, axis=0)


def zero_state():
    row, block = jnp.zeros((1, 128), F32), jnp.zeros((HEAD, 128), F32)
    return [(row, row, row, block, block, block) for _ in range(2)]


def fetch(source, buffer, sem, list_ref, group):
    for u in range(UNROLL):
        yield pltpu.make_async_copy(
            source.at[list_ref[group * UNROLL + u] % SLOTS], buffer.at[lax.rem(group, 2), u], sem.at[lax.rem(group, 2), u])


def query_kernel(list_ref, count_ref, q_ref, g_ref, kv_hbm, attn_ref, grad_ref, aux_ref, right, buffer, sem):
    count = count_ref[0]
    groups = (count + UNROLL - 1) // UNROLL
    for copy in fetch(kv_hbm, buffer, sem, list_ref, 0):
        copy.start()
    for x in range(BLK):
        right[x] = spread(q_ref[x], g_ref[x])

    def body(group, state):
        @pl.when(group + 1 < groups)
        def _():
            for copy in fetch(kv_hbm, buffer, sem, list_ref, group + 1):
                copy.start()

        for copy in fetch(kv_hbm, buffer, sem, list_ref, group):
            copy.wait()
        tiles = []
        for u in range(UNROLL):
            t = group * UNROLL + u
            tiles.append(query_tile(buffer[lax.rem(group, 2), u], right[list_ref[t] // SLOTS]))
        for u in range(UNROLL):
            t = group * UNROLL + u
            x = list_ref[t] // SLOTS
            before = list_ref[jnp.maximum(t - 1, 0)] // SLOTS
            reset = jnp.where((t == 0) | (before != x), NEG, 0.0).astype(F32)
            skip = jnp.where(t < count, 0.0, NEG).astype(F32)
            state = query_merge(state, tiles[u], reset, skip)
            rows, grads, aux = query_result(state)
            attn_ref[x] = rows
            grad_ref[x] = grads
            aux_ref[x] = aux
        return state

    lax.fori_loop(0, groups, body, zero_state())


def key_kernel(list_ref, count_ref, k_ref, v_ref, aux_all, qg_hbm, dk_ref, dv_ref, left, buffer, aux_buf, sem, aux_sem):
    count = count_ref[0]
    groups = (count + UNROLL - 1) // UNROLL

    def copies(group):
        yield from fetch(qg_hbm, buffer, sem, list_ref, group)
        yield from fetch(aux_all, aux_buf, aux_sem, list_ref, group)

    for copy in copies(0):
        copy.start()
    for y in range(BLK):
        left[y] = jnp.concatenate([k_ref[y], v_ref[y]], axis=0).T

    def body(group, state):
        @pl.when(group + 1 < groups)
        def _():
            for copy in copies(group + 1):
                copy.start()

        for copy in copies(group):
            copy.wait()
        terms = []
        for u in range(UNROLL):
            t = group * UNROLL + u
            terms.append(key_tile(left[list_ref[t] // SLOTS], buffer[lax.rem(group, 2), u], aux_buf[lax.rem(group, 2), u]))
        for u in range(UNROLL):
            t = group * UNROLL + u
            y = list_ref[t] // SLOTS
            before = list_ref[jnp.maximum(t - 1, 0)] // SLOTS
            keep = jnp.where((t == 0) | (before != y), 0.0, 1.0).astype(F32)
            use = jnp.where(t < count, 1.0, 0.0).astype(F32)
            state = tuple(x * keep + z * use for x, z in zip(state, terms[u]))
            dk_ref[y] = (state[0] * SCALE).astype(BF16)
            dv_ref[y] = state[1].astype(BF16)
        return state

    zero = jnp.zeros((64, 128), F32)
    lax.fori_loop(0, groups, body, (zero, zero))


def key_tile(left, qg, aux):
    right = spread(qg[:64], qg[64:])
    both = dot(left, right)
    lse = jnp.concatenate([aux[0:1], aux[1:2]], axis=1)
    delta = jnp.concatenate([aux[2:3], aux[3:4]], axis=1)
    prob = jnp.exp2((both[:, :256] - lse) * RATE)
    change = (prob * (both[:, 256:] - delta)).astype(BF16)
    term_k = dot_nt(right[:64, :256], change)
    term_v = dot_nt(right[64:, 256:], prob.astype(BF16))
    return term_k, term_v


def share_kernel(attn_ref, w_ref, aux_ref, out_ref, all_ref, local_sem, send_sem, recv_sem, outgoing, incoming):
    coords = place()
    y, z, core, hd, device = coords
    gather = Gather(all_ref, send_sem, recv_sem, coords)
    rows_a, rows_b = gather.own()
    copies = [
        pltpu.make_async_copy(aux_ref.at[pl.ds(0, PART_A)], rows_a, local_sem.at[0]),
        pltpu.make_async_copy(aux_ref.at[pl.ds(PART_A, PART_B)], rows_b, local_sem.at[1]),
    ]
    for copy in copies:
        copy.start()
    partners = [device(y, z, core, (hd + hop) % NX) for hop in range(1, NX)]
    meet(gather.peers() + partners)
    for copy in copies:
        copy.wait()
    steps = gather.steps()
    for step in steps[:3]:
        step()

    def project(a, carry):
        part = lax.dot_general(attn_ref[a], w_ref[...], (((0,), (0,)), ((), ())), preferred_element_type=F32).astype(BF16)
        for x in range(NX):
            outgoing[x, a] = part[32 * x:32 * x + 32]
        return carry

    lax.fori_loop(0, BLK, project, 0)
    legs = []
    for hop in range(1, NX):
        to = (hd + hop) % NX
        leg = pltpu.make_async_remote_copy(
            src_ref=outgoing.at[to], dst_ref=incoming.at[hop - 1], send_sem=send_sem.at[Gather.SEMS + hop],
            recv_sem=recv_sem.at[Gather.SEMS + hop], device_id=partners[hop - 1], device_id_type=MESH)
        leg.start()
        legs.append(leg)
    for step in steps[3:]:
        step()
    for leg in legs:
        leg.wait()

    def total(a, carry):
        value = outgoing[hd, a].astype(F32)
        for hop in range(NX - 1):
            value += incoming[hop, a].astype(F32)
        out_ref[a] = value.astype(BF16)
        return carry

    lax.fori_loop(0, BLK, total, 0)


def tile_list(pair_list):
    me = lax.axis_index("blk")
    first, second = pair_list[0], pair_list[1]
    count_all = first.shape[0]
    mine = count_all // lax.axis_size("blk")
    start = me * BLK
    own = start + jnp.arange(BLK, dtype=jnp.int32)
    out_first = lax.dynamic_slice_in_dim(first, me * mine, mine)
    out_second = lax.dynamic_slice_in_dim(second, me * mine, mine)
    near = jnp.concatenate([own, out_first, second])
    far = jnp.concatenate([own, out_second, first])
    inside = (near >= start) & (near < start + BLK)
    number = near.shape[0]
    order = jnp.where(inside, near - start, BLK) * 4096 + jnp.arange(number, dtype=jnp.int32)
    rank = jnp.sum((order[None, :] < order[:, None]).astype(jnp.int32), axis=1)
    rank = jnp.where(inside, rank, LIST)
    value = (near - start) * SLOTS + slot_of(far)
    hit = rank[None, :] == jnp.arange(LIST, dtype=jnp.int32)[:, None]
    entries = jnp.sum(jnp.where(hit, value[None, :], 0), axis=1)
    count = jnp.sum(inside.astype(jnp.int32))
    entries = jnp.where(jnp.arange(LIST) < count, entries, (BLK - 1) * SLOTS)
    return entries.astype(jnp.int32), count[None].astype(jnp.int32)


def local(queries, keys, values, out_weight, out_grad, pair_list):
    entries, count = tile_list(pair_list)
    grads = jnp.einsum("bro,fo->bfr", out_grad, out_weight, preferred_element_type=F32).astype(BF16)
    kv_all, qg_all = gather_all(keys, values, queries, grads)
    smem = pl.BlockSpec(memory_space=pltpu.SMEM)
    vmem = pl.BlockSpec(memory_space=pltpu.VMEM)
    anywhere = pl.BlockSpec(memory_space=pl.ANY)
    sem = pltpu.SemaphoreType.DMA
    half = jax.ShapeDtypeStruct((BLK, 64, 128), BF16)
    attn, grad_q, aux = pl.pallas_call(
        query_kernel,
        out_shape=(half, half, jax.ShapeDtypeStruct((BLK, 8, 128), F32)),
        in_specs=[smem, smem, vmem, vmem, anywhere], out_specs=(vmem,) * 3,
        scratch_shapes=[pltpu.VMEM((BLK, 128, 512), BF16), pltpu.VMEM((2, UNROLL, 128, 128), BF16), sem((2, UNROLL))],
        compiler_params=pltpu.CompilerParams(vmem_limit_bytes=32 * 2**20),
        name="query_side",
    )(entries, count, queries, grads, kv_all)
    out, aux_all = pl.pallas_call(
        share_kernel,
        out_shape=(jax.ShapeDtypeStruct((BLK, 32, 256), BF16), jax.ShapeDtypeStruct((SLOTS, 8, 128), F32)),
        in_specs=[vmem, vmem, vmem], out_specs=(vmem, anywhere),
        scratch_shapes=[sem((2,)), sem((Gather.SEMS + NX,)), sem((Gather.SEMS + NX,)), pltpu.VMEM((NX, BLK, 32, 256), BF16),
                        pltpu.VMEM((NX - 1, BLK, 32, 256), BF16)],
        compiler_params=pltpu.CompilerParams(collective_id=1, has_side_effects=True, vmem_limit_bytes=32 * 2**20),
        name="share_rows",
    )(attn, out_weight, aux)
    grad_k, grad_v = pl.pallas_call(
        key_kernel,
        out_shape=(half, half),
        in_specs=[smem, smem, vmem, vmem, anywhere, anywhere], out_specs=(vmem,) * 2,
        scratch_shapes=[pltpu.VMEM((BLK, 128, 128), BF16), pltpu.VMEM((2, UNROLL, 128, 128), BF16),
                        pltpu.VMEM((2, UNROLL, 8, 128), F32), sem((2, UNROLL)), sem((2, UNROLL))],
        compiler_params=pltpu.CompilerParams(vmem_limit_bytes=32 * 2**20),
        name="key_side",
    )(entries, count, keys, values, aux_all, qg_all)
    return out, grad_q, grad_k, grad_v


def solution(mesh):
    blocks, weight = P("blk", "hd", None), P("hd", None)
    return jax.shard_map(
        local, mesh=mesh,
        in_specs=(blocks, blocks, blocks, weight, P("blk", None, None), P()),
        out_specs=(blocks,) * 4, check_vma=False)
```

time: 682 us -> 405 us (0.59); the launches traced: 669 us -> 402 us
  Pallas kernels: 0 us -> 392 us
  waiting for transfers between devices: 200 us -> 0 us
  other arithmetic: 147 us -> 3.61 us
  blocking collectives: 121 us -> 0 us
  local copies, waits for them, and re-layouts: 91.3 us -> 3.7 us
  starting transfers between devices: 65 us -> 0 us
  matrix products: 28.9 us -> 1.9 us
  between operations: 15.2 us -> 0.76 us
    pallas_call x0 -> x4, Pallas kernels: none -> 392 us  [the longest x1 307 us: gather_all(): pl.pallas_call(gather_kernel, out_shape=(shape, shape), in_specs=[anywher...]
    all_to_all x9 -> x0, waiting for transfers between devices: 200 us -> none  [the longest x1 87.6 us: local(): lax.all_to_all(back_out, 'blk', split_axis=0, concat_axis=0, tiled=True)]
    all_to_all x2 -> x0, blocking collectives: 121 us -> none  [the longest x1 64.3 us: local(): lax.all_to_all(pick_rows(values, row_block), 'blk', split_axis=0, concat_...]
    scatter-add x9 -> x0, other arithmetic: 95.5 us -> none  [the longest x3 40.8 us: home_sum(): jax.ops.segment_sum(terms.astype(jnp.float32), row_block, num_segments=bl...]
    all_to_all x9 -> x0, starting transfers between devices: 64.7 us -> none  [the longest x1 10.6 us: local(): lax.all_to_all(pick_rows(row_delta, row_block), 'blk', split_axis=0, conc...]
    gather x20 -> x0, local copies, waits for them, and re-layouts: 34.2 us -> none  [the longest x6 10.9 us: pick_rows(): return jnp.take(padded, index, axis=0)]
    dot_general x36 -> x1, matrix products: 28.9 us -> 1.9 us  [local(): jnp.einsum('bro,fo->bfr', out_grad, out_weight, preferred_element_type=F32)]
    scatter x5 -> x0, local copies, waits for them, and re-layouts: 23 us -> none  [the longest x3 14 us: placed(): return jnp.zeros((slots_all,) + terms.shape[1:], jnp.bfloat16).at[dest_ro...]
  transfers between devices with their start and end apart: 10 -> 0, of which waited for: 6 -> 0; matrix products, arithmetic and copies ran while one was open for 35% -> 0% of each run, Pallas kernels for 0% -> 0%
where the time goes in v1:
time: 405 us; the launch traced here: 402 us
  Pallas kernels  392 us (97%)
    pallas_call x1, Pallas kernels, gather_all(): pl.pallas_call(gather_kernel, out_shape=(shape, shape), in_specs=[anywher...  307 us
    pallas_call x1, Pallas kernels, local(): pl.pallas_call(share_kernel, out_shape=(jax.ShapeDtypeStruct((BLK, 32, 25...  33.8 us
    pallas_call x1, Pallas kernels, local(): pl.pallas_call(query_kernel, out_shape=(half, half, jax.ShapeDtypeStruct(...  28.1 us
    pallas_call x1, Pallas kernels, local(): pl.pallas_call(key_kernel, out_shape=(half, half), in_specs=[smem, smem,...  23.4 us

profile of v1, /device:TPU:1, one launch (start us, length us, event | category | flops | bytes accessed | tf_op | source)
XLA Modules:
  0.0 402.1 jit_solution(1098484511312616906)
XLA Ops:
  0.6 0.0 copy-start
  0.7 0.8 fusion.10
  1.5 0.1 dynamic-slice_bitcast_fusion
  1.6 0.1 concatenate.63
  1.7 0.1 concatenate.60
  1.7 0.6 convert_reduce_fusion.1
  2.4 0.1 iota_add_fusion
  2.4 2.0 convert_reduce_fusion
  4.4 0.3 select_reduce_fusion
  4.7 0.6 compare_select_fusion.list_ref
  5.4 0.0 copy-done
  5.4 1.9 fusion.g_ref
  7.3 306.9 %gather_rows.1 = (bf16[1024,128,128]{2,1,0:T(8,128)(2,1)}, bf16[1024,128,128]{2,1,0:T(8,128)(2,1)}) custom-call(bf16[16,64,128]{2,1,0:T(8,128)(2,1)} %k_ref.3, bf16[16,64,128]{2,1,0:T(8,128)(2,1)} %v_ref.3, bf16[16,64,128]{2,1,0:T(8,128)(2,1)} %q_ref.3, bf16[16,64,128]{2,1,0:T(8,128)(2,1)} %fusion.g_ref), custom_call_target="tpu_custom_call" | custom-call | tf_op jit(solution)/shard_map/gather_rows/pallas_call | solution.py:193
  314.2 0.0 copy-start.2
  314.2 0.9 copy-done.2
  315.1 0.9 copy-done.3
  316.1 28.1 %query_side.1 = (bf16[16,64,128]{2,1,0:T(8,128)(2,1)S(1)}, bf16[16,64,128]{2,1,0:T(8,128)(2,1)}, f32[16,8,128]{2,1,0:T(8,128)S(1)}) custom-call(s32[192]{0:T(256)S(1)} %compare_select_fusion.list_ref, s32[1]{0:T(128)} %bitcast.4.count_ref, bf16[16,64,128]{2,1,0:T(8,128)(2,1)S(1)} %copy-done.3, bf16[16,64,128]{2,1,0:T(8,128)(2,1)S(1)} %copy-done.2, ...), custom_call_target="tpu_custom_call" | custom-call | tf_op jit(solution)/shard_map/query_side/pallas_call | solution.py:444
  344.2 0.0 copy-done.6
  344.2 33.8 %share_rows.1 = (bf16[16,32,256]{2,1,0:T(8,128)(2,1)S(1)}, f32[1024,8,128]{2,1,0:T(8,128)S(1)}) custom-call(bf16[16,64,128]{2,1,0:T(8,128)(2,1)S(1)} %get-tuple-element.14.attn_ref, bf16[64,256]{1,0:T(8,128)(2,1)S(1)} %copy-done.6, f32[16,8,128]{2,1,0:T(8,128)S(1)} %get-tuple-element.15.aux_ref), custom_call_target="tpu_custom_call" | custom-call | tf_op jit(solution)/shard_map/share_rows/pallas_call | solution.py:452
  378.0 0.0 copy-done.4
  378.0 0.0 copy-done.5
  378.0 0.0 copy-start.1
  378.0 23.4 %key_side.1 = (bf16[16,64,128]{2,1,0:T(8,128)(2,1)}, bf16[16,64,128]{2,1,0:T(8,128)(2,1)}) custom-call(s32[192]{0:T(256)S(1)} %compare_select_fusion.list_ref, s32[1]{0:T(128)} %bitcast.4.count_ref, bf16[16,64,128]{2,1,0:T(8,128)(2,1)S(1)} %copy-done.4, bf16[16,64,128]{2,1,0:T(8,128)(2,1)S(1)} %copy-done.5, f32[1024,8,128]{2,1,0:T(8,128)S(1)} %get-tuple-element.18.aux_all, ...), custom_call_target="tpu_custom_call" | custom-call | tf_op jit(solution)/shard_map/key_side/pallas_call | solution.py:461
  401.4 0.7 copy.11
  (7 shorter events, 0.0 us)
Async XLA Ops:
  0.6 4.7 %copy-start = (bf16[16,128,256]{2,1,0:T(8,128)(2,1)S(1)}, bf16[16,128,256]{2,1,0:T(8,128)(2,1)}, u32[]{:S(2)}) copy-start(bf16[16,128,256]{2,1,0:T(8,128)(2,1)} %param.10) | copy-start | bytes 3145732
  314.2 1.0 copy-start.2
  315.1 0.9 copy-start.3
  316.1 28.1 %copy-start.6 = (bf16[64,256]{1,0:T(8,128)(2,1)S(1)}, bf16[64,256]{1,0:T(8,128)(2,1)}, u32[]{:S(2)}) copy-start(bf16[64,256]{1,0:T(8,128)(2,1)} %w_ref.1) | copy-start | bytes 98308
  316.1 61.9 %copy-start.4 = (bf16[16,64,128]{2,1,0:T(8,128)(2,1)S(1)}, bf16[16,64,128]{2,1,0:T(8,128)(2,1)}, u32[]{:S(2)}) copy-start(bf16[16,64,128]{2,1,0:T(8,128)(2,1)} %k_ref.3) | copy-start | bytes 786436
  316.1 61.9 %copy-start.5 = (bf16[16,64,128]{2,1,0:T(8,128)(2,1)S(1)}, bf16[16,64,128]{2,1,0:T(8,128)(2,1)}, u32[]{:S(2)}) copy-start(bf16[16,64,128]{2,1,0:T(8,128)(2,1)} %v_ref.3) | copy-start | bytes 786436
  378.0 24.1 %copy-start.1 = (bf16[16,128,256]{2,1,0:T(8,128)(2,1)S(1)}, bf16[16,128,256]{2,1,0:T(8,128)(2,1)}, u32[]{:S(2)}) copy-start(bf16[16,128,256]{2,1,0:T(8,128)(2,1)} %param.10) | copy-start | bytes 3145732

commit v2 on v1

v2 whole, which is shorter than its diff:
```python
import functools

import jax
import jax.numpy as jnp
from jax import lax
from jax.experimental import pallas as pl
from jax.experimental.pallas import tpu as pltpu
from jax.sharding import PartitionSpec as P

MESH = pl.DeviceIdType.MESH
HEAD = 32
NY, NZ, NX = 4, 8, 4
BLK = 16
COLUMN = 2 * NZ * BLK
UNROLL = 4
NEG = -1e30
RATE = HEAD**-0.5 * 1.4426950408889634
SCALE = HEAD**-0.5
F32 = jnp.float32
BF16 = jnp.bfloat16
VMEM_LIMIT = 60 * 2**20


def place():
    blk, hd = lax.axis_index("blk"), lax.axis_index("hd")
    core, z, y = blk % 2, (blk // 2) % NZ, blk // (2 * NZ)

    def device(yy, zz, cc, xx):
        return ((yy * NZ + zz) * 2 + cc, xx)

    return y, z, core, hd, device


def meet(peers):
    barrier = pltpu.get_barrier_semaphore()
    for peer in peers:
        pl.semaphore_signal(barrier, inc=1, device_id=peer, device_id_type=MESH)
    pl.semaphore_wait(barrier, len(peers))


class Sems:
    def __init__(self, send, recv):
        self.send, self.recv, self.used = send, recv, 0

    def take(self, count):
        self.used += count
        return self.used - count

    def copy(self, source, target, peer, sem):
        return pltpu.make_async_remote_copy(
            src_ref=source, dst_ref=target, send_sem=self.send.at[sem], recv_sem=self.recv.at[sem],
            device_id=peer, device_id_type=MESH)


class Ring:
    def __init__(self, buffer, coords, sems, pieces):
        self.buffer, self.sems, self.pieces = buffer, sems, pieces
        y, z, core, hd, device = coords
        self.z, self.core = z, core
        self.peer = (device(y, (z + 1) % NZ, core, hd), device(y, (z + NZ - 1) % NZ, core, hd))
        self.twin = device(y, z, 1 - core, hd)
        self.size = BLK // pieces
        self.leg_sem, self.twin_sem = sems.take(8 * pieces), sems.take(8 * pieces)
        self.sent = []

    def peers(self):
        return [*self.peer, self.twin]

    def rows(self, z, core, start, count):
        return self.buffer.at[pl.ds((z * 2 + core) * BLK + start, count)]

    def leg(self, piece, step, way, arriving):
        hop = step + 1 if arriving else step
        z = (self.z - hop + NZ) % NZ if way == 0 else (self.z + hop) % NZ
        start, count = piece * self.size, self.size
        if step == 3:
            count //= 2
            start += way * count
        rows = self.rows(z, self.core, start, count)
        return self.sems.copy(rows, rows, self.peer[way], self.leg_sem + (piece * 4 + step) * 2 + way)

    def pass_on(self, piece, hop, core):
        rows = self.rows((self.z + hop + NZ) % NZ, core, piece * self.size, self.size)
        return self.sems.copy(rows, rows, self.twin, self.twin_sem + piece * 8 + hop % NZ)

    def go(self, copy):
        copy.start()
        self.sent.append(copy)

    def start(self):
        for piece in range(self.pieces):
            for way in (0, 1):
                self.go(self.leg(piece, 0, way, False))
        for piece in range(self.pieces):
            self.go(self.pass_on(piece, 0, self.core))

    def advance(self, step):
        for piece in range(self.pieces):
            for way in (0, 1):
                self.leg(piece, step, way, True).wait_recv()
                if step < 3:
                    self.go(self.leg(piece, step + 1, way, False))
                    self.go(self.pass_on(piece, -1 - step if way == 0 else 1 + step, self.core))
            if step == 3:
                self.go(self.pass_on(piece, 4, self.core))

    def arrive(self):
        for piece in range(self.pieces):
            for hop in range(NZ):
                self.pass_on(piece, hop, 1 - self.core).wait_recv()

    def drain(self):
        for copy in self.sent:
            copy.wait_send()


class Cross:
    def __init__(self, send, relay, recv, cap, coords, sems):
        self.send, self.relay, self.recv, self.cap, self.sems = send, relay, recv, cap, sems
        y, z, core, hd, device = coords
        self.peer = (device((y + 1) % NY, z, core, hd), device((y + NY - 1) % NY, z, core, hd))
        self.sem = sems.take(6)
        self.sent = []

    def peers(self):
        return [*self.peer]

    def first(self, way):
        half = self.cap // 2
        return self.sems.copy(
            self.send.at[pl.ds(self.cap + way * half, half)], self.relay.at[pl.ds(way * half, half)], self.peer[way], self.sem + way)

    def second(self, way):
        half = self.cap // 2
        return self.sems.copy(
            self.relay.at[pl.ds(way * half, half)], self.recv.at[pl.ds(2 * self.cap + way * half, half)], self.peer[way],
            self.sem + 2 + way)

    def direct(self, way):
        return self.sems.copy(
            self.send.at[pl.ds(2 * way * self.cap, self.cap)],
            self.recv.at[pl.ds((3 - 2 * way) * self.cap, self.cap)], self.peer[way], self.sem + 4 + way)

    def go(self, copy):
        copy.start()
        self.sent.append(copy)

    def pack(self, column, list_ref):
        def move(hop, target, base):
            def body(step, carry):
                for u in range(4):
                    row = step * 4 + u
                    target[base + row] = column[list_ref[hop * self.cap + row]]
                return carry

            lax.fori_loop(0, self.cap // 4, body, 0)

        move(2, self.send, self.cap)
        for way in (0, 1):
            self.go(self.first(way))
        move(1, self.send, 0)
        self.go(self.direct(0))
        move(3, self.send, 2 * self.cap)
        self.go(self.direct(1))
        move(0, self.recv, 0)

    def relay_on(self):
        for way in (0, 1):
            self.first(way).wait_recv()
            self.go(self.second(way))

    def arrive(self):
        for way in (0, 1):
            self.direct(way).wait_recv()
            self.second(way).wait_recv()

    def drain(self):
        for copy in self.sent:
            copy.wait_send()


def spread(first, second):
    parts = (first[:HEAD], first[HEAD:], second[:HEAD], second[HEAD:])
    zero = jnp.zeros((HEAD, 128), first.dtype)
    rows = [jnp.concatenate([part if col == row else zero for col in range(4)], axis=1) for row, part in enumerate(parts)]
    return jnp.concatenate(rows, axis=0)


def diagonal(full, top):
    return full[top:top + HEAD, :128], full[top + HEAD:top + 2 * HEAD, 128:]


def dot(a, b):
    return jnp.dot(a, b, preferred_element_type=F32)


def dot_nt(a, b):
    return lax.dot_general(a, b, (((1,), (1,)), ((), ())), preferred_element_type=F32)


def query_tile(kv, right):
    both = dot(kv.T, right)
    scores, prob_grad = both[:, :256], both[:, 256:]
    top = jnp.max(scores, axis=0, keepdims=True)
    expo = jnp.exp2((scores - top) * RATE)
    total = jnp.sum(expo, axis=0, keepdims=True)
    weighed = jnp.sum(expo * prob_grad, axis=0, keepdims=True)
    mean = weighed / total
    change = (expo * (prob_grad - mean)).astype(BF16)
    by_expo = dot(kv, expo.astype(BF16))
    by_change = dot(kv[:64], change)
    heads = []
    for h in range(2):
        cols = slice(128 * h, 128 * h + 128)
        b = diagonal(by_expo, 0)[h]
        o = diagonal(by_expo, 64)[h]
        a = diagonal(by_change, 0)[h] + mean[:, cols] * b
        heads.append((top[:, cols], total[:, cols], weighed[:, cols], o, a, b))
    return heads


def query_merge(old, new, skip):
    merged = []
    for (m0, *acc), (m1, *add) in zip(old, new):
        m1 = m1 + skip
        m = jnp.maximum(m0, m1)
        w0, w1 = jnp.exp2((m0 - m) * RATE), jnp.exp2((m1 - m) * RATE)
        merged.append((m, *[x * w0 + y * w1 for x, y in zip(acc, add)]))
    return merged


def query_result(state):
    rows, grads, stats = [], [], []
    for m, total, weighed, o, a, b in state:
        inverse = 1.0 / total
        delta = weighed * inverse
        rows.append((o * inverse).astype(BF16))
        grads.append(((a - delta * b) * (inverse * SCALE)).astype(BF16))
        stats.append((m + jnp.log2(total) * (1.0 / RATE), delta))
    aux = [stats[0][0], stats[1][0], stats[0][1], stats[1][1], jnp.zeros((4, 128), F32)]
    return jnp.concatenate(rows + grads, axis=0), jnp.concatenate(aux, axis=0)


def pack_state(state):
    rows = [x for head in state for x in head[:3]] + [jnp.zeros((2, 128), F32)]
    return jnp.concatenate(rows, axis=0), jnp.concatenate([x for head in state for x in head[3:]], axis=0)


def load_state(rows, blocks):
    return [
        (*[rows[3 * h + i:3 * h + i + 1] for i in range(3)], *[blocks[96 * h + 32 * i:96 * h + 32 * i + 32] for i in range(3)])
        for h in range(2)
    ]


def key_tile(left, qg, aux):
    right = spread(qg[:64], qg[64:])
    both = dot(left, right)
    lse = jnp.concatenate([aux[0:1], aux[1:2]], axis=1)
    delta = jnp.concatenate([aux[2:3], aux[3:4]], axis=1)
    prob = jnp.exp2((both[:, :256] - lse) * RATE)
    change = (prob * (both[:, 256:] - delta)).astype(BF16)
    term_k = dot_nt(right[:64, :256], change)
    term_v = dot_nt(right[64:, 256:], prob.astype(BF16))
    return jnp.concatenate([term_k, term_v], axis=0)


def kernel(cap, far, send_list, tile_list, last_list, count_ref, q_ref, k_ref, v_ref, w_ref, og_ref,
           out_ref, dq_ref, dk_ref, dv_ref,
           col_kv, col_qg, col_aux, send_kv, send_qg, send_aux, relay_kv, relay_qg, relay_aux, recv_kv, recv_qg, recv_aux,
           right, left, self_rows, self_blocks, both_t, aux_t, aux_own, attn_own, self_terms,
           outgoing, incoming, send_sem, recv_sem):
    coords = place()
    y, z, core, hd, device = coords
    own = (z * 2 + core) * BLK
    sems = Sems(send_sem, recv_sem)
    ring_kv, ring_qg, ring_aux = (Ring(buffer, coords, sems, pieces) for buffer, pieces in ((col_kv, 2), (col_qg, 2), (col_aux, 1)))
    cross_kv = Cross(send_kv, relay_kv, recv_kv, cap, coords, sems)
    shared = cap > 32
    if shared:
        send_qg = send_kv
    cross_qg = Cross(send_qg, relay_qg, recv_qg, cap, coords, sems)
    cross_aux = Cross(send_aux, relay_aux, recv_aux, cap, coords, sems)
    partners = [device(y, z, core, (hd + hop) % NX) for hop in range(1, NX)]
    count = count_ref[0]

    def fill_kv(x, carry):
        kv = jnp.concatenate([k_ref[x], v_ref[x]], axis=0)
        col_kv[own + x] = kv
        return carry

    lax.fori_loop(0, BLK, fill_kv, 0)
    meet(ring_kv.peers() + cross_kv.peers() + partners)
    ring_kv.start()

    def fill_qg(x, carry):
        g = dot_nt(w_ref[...], og_ref[x]).astype(BF16)
        q = q_ref[x]
        col_qg[own + x] = jnp.concatenate([q, g], axis=0)
        right[x] = spread(q, g)
        left[x] = jnp.concatenate([k_ref[x], v_ref[x]], axis=0).T
        return carry

    lax.fori_loop(0, BLK, fill_qg, 0)

    def self_query(group, carry):
        for u in range(UNROLL):
            x = group * UNROLL + u
            state = query_tile(jnp.concatenate([k_ref[x], v_ref[x]], axis=0), right[x])
            self_rows[x], self_blocks[x] = pack_state(state)
            both_t[far + x], aux_t[far + x] = query_result(state)
        return carry

    ring_kv.advance(0)
    lax.fori_loop(0, 2, self_query, 0)
    ring_kv.advance(1)
    lax.fori_loop(2, 4, self_query, 0)
    ring_kv.advance(2)
    ring_qg.start()
    ring_kv.advance(3)
    ring_kv.arrive()
    cross_kv.pack(col_kv, send_list)
    ring_qg.advance(0)
    cross_kv.relay_on()
    ring_qg.advance(1)
    ring_qg.advance(2)
    ring_qg.advance(3)
    ring_qg.arrive()
    if shared:
        cross_kv.arrive()
        cross_kv.drain()
    cross_qg.pack(col_qg, send_list)
    if not shared:
        cross_kv.arrive()
        cross_kv.drain()

    def entry(t):
        value = tile_list[t]
        x = value // 1024
        before = tile_list[jnp.maximum(t - 1, 0)] // 1024
        return value % 1024, x, (t == 0) | (before != x)

    def far_query(group, state):
        tiles = []
        for u in range(UNROLL):
            row, x, _ = entry(group * UNROLL + u)
            tiles.append(query_tile(recv_kv[row], right[x]))
        for u in range(UNROLL):
            t = group * UNROLL + u
            _, x, fresh = entry(t)
            base = load_state(self_rows[x], self_blocks[x])
            state = [tuple(jnp.where(fresh, b, s) for b, s in zip(head0, head1)) for head0, head1 in zip(base, state)]
            skip = jnp.where(t < count, 0.0, NEG).astype(F32)
            state = query_merge(state, tiles[u], skip)
            both_t[t], aux_t[t] = query_result(state)
        return state

    row, block = jnp.zeros((1, 128), F32), jnp.zeros((HEAD, 128), F32)
    state = [(row, row, row, block, block, block) for _ in range(2)]
    groups = far // UNROLL
    state = lax.fori_loop(0, groups // 2, far_query, state)
    cross_qg.relay_on()
    lax.fori_loop(groups // 2, groups, far_query, state)

    def finish_query(x, carry):
        t = last_list[x]
        aux = aux_t[t]
        aux_own[x] = aux
        col_aux[own + x] = aux
        both = both_t[t]
        dq_ref[x] = both[64:]
        attn_own[x] = both[:64]
        return carry

    lax.fori_loop(0, BLK, finish_query, 0)
    ring_aux.start()

    def project(a, carry):
        part = lax.dot_general(attn_own[a], w_ref[...], (((0,), (0,)), ((), ())), preferred_element_type=F32).astype(BF16)
        for x in range(NX):
            outgoing[x, a] = part[32 * x:32 * x + 32]
        return carry

    lax.fori_loop(0, BLK, project, 0)
    legs = []
    partner_sem = sems.take(NX - 1)
    for hop in range(1, NX):
        leg = sems.copy(outgoing.at[(hd + hop) % NX], incoming.at[hop - 1], partners[hop - 1], partner_sem + hop - 1)
        leg.start()
        legs.append(leg)

    def self_key(group, carry):
        for u in range(UNROLL):
            x = group * UNROLL + u
            terms = key_tile(left[x], col_qg[own + x], aux_own[x])
            self_terms[x] = terms
            both_t[far + x] = terms.astype(BF16)
        return carry

    ring_aux.advance(0)
    lax.fori_loop(0, 2, self_key, 0)
    ring_aux.advance(1)
    lax.fori_loop(2, 4, self_key, 0)
    ring_aux.advance(2)
    ring_aux.advance(3)
    ring_aux.arrive()
    cross_aux.pack(col_aux, send_list)
    cross_aux.relay_on()
    cross_aux.arrive()
    cross_qg.arrive()

    def far_key(group, state):
        tiles = []
        for u in range(UNROLL):
            row, x, _ = entry(group * UNROLL + u)
            tiles.append(key_tile(left[x], recv_qg[row], recv_aux[row]))
        for u in range(UNROLL):
            t = group * UNROLL + u
            _, x, fresh = entry(t)
            use = jnp.where(t < count, 1.0, 0.0).astype(F32)
            state = jnp.where(fresh, self_terms[x], state) + tiles[u] * use
            both_t[t] = state.astype(BF16)
        return state

    lax.fori_loop(0, groups, far_key, jnp.zeros((128, 128), F32))

    def finish_key(x, carry):
        terms = both_t[last_list[x]]
        dk_ref[x] = (terms[:64].astype(F32) * SCALE).astype(BF16)
        dv_ref[x] = terms[64:]
        return carry

    lax.fori_loop(0, BLK, finish_key, 0)
    for leg in legs:
        leg.wait()

    def total(a, carry):
        value = outgoing[hd, a].astype(F32)
        for hop in range(NX - 1):
            value += incoming[hop, a].astype(F32)
        out_ref[a] = value.astype(BF16)
        return carry

    lax.fori_loop(0, BLK, total, 0)
    for part in (ring_kv, ring_qg, ring_aux, cross_qg, cross_aux):
        part.drain()


def run(cap, far, number, send_list, tile_list, last_list, count, *arrays):
    smem = pl.BlockSpec(memory_space=pltpu.SMEM)
    vmem = pl.BlockSpec(memory_space=pltpu.VMEM)
    sem = pltpu.SemaphoreType.DMA
    half = jax.ShapeDtypeStruct((BLK, 64, 128), BF16)

    def wide(rows, second=None):
        second = rows if second is None else second
        return [pltpu.VMEM((rows, 128, 128), BF16), pltpu.VMEM((second, 128, 128), BF16), pltpu.VMEM((rows, 8, 128), F32)]

    scratch = [
        *wide(COLUMN), *wide(3 * cap, 3 * cap if cap <= 32 else 8), *wide(cap), *wide(4 * cap),
        pltpu.VMEM((BLK, 128, 512), BF16), pltpu.VMEM((BLK, 128, 128), BF16),
        pltpu.VMEM((BLK, 8, 128), F32), pltpu.VMEM((BLK, 192, 128), F32),
        pltpu.VMEM((far + BLK, 128, 128), BF16), pltpu.VMEM((far + BLK, 8, 128), F32),
        pltpu.VMEM((BLK, 8, 128), F32), pltpu.VMEM((BLK, 64, 128), BF16),
        pltpu.VMEM((BLK, 128, 128), F32),
        pltpu.VMEM((NX, BLK, 32, 256), BF16), pltpu.VMEM((NX - 1, BLK, 32, 256), BF16),
        sem((108,)), sem((108,)),
    ]
    return pl.pallas_call(
        functools.partial(kernel, cap, far),
        out_shape=(jax.ShapeDtypeStruct((BLK, 32, 256), BF16), half, half, half),
        in_specs=[smem] * 4 + [vmem] * 5, out_specs=(vmem,) * 4, scratch_shapes=scratch,
        compiler_params=pltpu.CompilerParams(collective_id=number, has_side_effects=True, vmem_limit_bytes=VMEM_LIMIT),
        name="attention",
    )(send_list[:, :cap].reshape(-1), tile_list[:far], last_list, count, *arrays)


def before(marks):
    rows, length = marks.shape
    cut = marks.astype(BF16).reshape(rows, length // 128, 128)
    lower = (jnp.arange(128)[:, None] < jnp.arange(128)[None, :]).astype(BF16)
    inside = jnp.einsum("rsc,cd->rsd", cut, lower, preferred_element_type=F32)
    sums = jnp.sum(cut.astype(F32), axis=2)
    ahead = jnp.arange(length // 128)[:, None] < jnp.arange(length // 128)[None, :]
    starts = jnp.sum(jnp.where(ahead[None], sums[:, :, None], 0.0), axis=1)
    return (inside + starts[:, :, None]).astype(jnp.int32).reshape(rows, length), jnp.sum(sums, axis=1).astype(jnp.int32)


def lists(pair_list, cap, far):
    me = lax.axis_index("blk")
    y, rest = me // (2 * NZ), me % (2 * NZ)
    near = jnp.concatenate([pair_list[0], pair_list[1]])
    away = jnp.concatenate([pair_list[1], pair_list[0]])
    near_dev, away_col = near // BLK, away // COLUMN
    hops = jnp.arange(NY, dtype=jnp.int32)
    asked = (near_dev[None] == ((y + hops) % NY * 2 * NZ + rest)[:, None]) & (away_col == y)[None]
    mine = near_dev == me
    source = mine[None] & (away_col[None] == ((y + hops) % NY)[:, None])
    at_block = mine[None] & ((near % BLK)[None] == jnp.arange(BLK, dtype=jnp.int32)[:, None])
    rank, sums = before(jnp.concatenate([asked, source, at_block], axis=0))
    place_of = jnp.arange(cap, dtype=jnp.int32)
    hit = asked[:, None] & (rank[:NY, None] == place_of[None, :, None])
    send_list = jnp.sum(jnp.where(hit, (away % COLUMN)[None, None], 0), axis=2)
    row = jnp.sum(jnp.where(source, rank[NY:2 * NY] + hops[:, None] * cap, 0), axis=0)
    counts = sums[2 * NY:]
    starts = jnp.sum(jnp.where(jnp.arange(BLK)[None, :] < jnp.arange(BLK)[:, None], counts[None, :], 0), axis=1)
    spot = jnp.sum(jnp.where(at_block, rank[2 * NY:] + starts[:, None], 0), axis=0)
    spot = jnp.where(mine, spot, far)
    value = near % BLK * 1024 + row
    chosen = spot[None] == jnp.arange(far, dtype=jnp.int32)[:, None]
    tile_list = jnp.sum(jnp.where(chosen, value[None], 0), axis=1)
    count = jnp.sum(counts)
    tile_list = jnp.where(jnp.arange(far) < count, tile_list, (BLK - 1) * 1024)
    last_list = jnp.where(counts > 0, starts + counts - 1, far + jnp.arange(BLK))
    i32 = jnp.int32
    return send_list.astype(i32), tile_list.astype(i32), last_list.astype(i32), count[None].astype(i32)


def most(pair_list):
    near = jnp.concatenate([pair_list[0], pair_list[1]]) // BLK
    away = jnp.concatenate([pair_list[1], pair_list[0]]) // COLUMN
    bins = jnp.arange(64 * NY, dtype=jnp.int32)
    counts = jnp.sum(((near * NY + away)[None] == bins[:, None]).astype(jnp.int32), axis=1)
    return jnp.max(counts), jnp.max(jnp.sum(counts.reshape(64, NY), axis=1))


def local(queries, keys, values, out_weight, out_grad, pair_list):
    arrays = (queries, keys, values, out_weight, out_grad)

    def branch(cap, far, number):
        return lambda: run(cap, far, number, *lists(pair_list, cap, far), *arrays)

    rows, tiles = most(pair_list)
    return lax.cond((rows <= 32) & (tiles <= 88), branch(32, 88, 0), branch(64, 160, 1))


def solution(mesh):
    blocks, weight = P("blk", "hd", None), P("hd", None)
    return jax.shard_map(
        local, mesh=mesh,
        in_specs=(blocks, blocks, blocks, weight, P("blk", None, None), P()),
        out_specs=(blocks,) * 4, check_vma=False)
```

time: 405 us -> 190 us (0.47)
  Pallas kernels: 392 us -> 175 us
    pallas_call x4 -> x1, Pallas kernels: 392 us -> 175 us  [run(): pl.pallas_call(functools.partial(kernel, cap, far), out_shape=(jax.ShapeD...]
where the time goes in v2:
time: 190 us; the launch traced here: 189 us
  Pallas kernels  175 us (92%)
  other arithmetic  6.65 us (4%)
  local copies, waits for them, and re-layouts  5.28 us (3%)
  between operations  1.98 us (1%)
    pallas_call x1, Pallas kernels, run(): pl.pallas_call(functools.partial(kernel, cap, far), out_shape=(jax.ShapeD...  175 us

profile of v2, /device:TPU:1, one launch (start us, length us, event | category | flops | bytes accessed | tf_op | source)
XLA Modules:
  0.0 189.5 jit_solution(8253797924344706247)
XLA Ops:
  0.6 0.8 fusion.66
  1.5 0.5 convert_reduce_fusion.4
  2.0 0.6 reduce_max.18
  3.3 0.1 reshape.1309
  3.4 0.1 reduce_sum.189
  3.5 0.6 reduce_max.19
  4.8 181.9 %conditional.1 = ((bf16[16,32,256]{2,1,0:T(8,128)(2,1)S(1)}, bf16[16,64,128]{2,1,0:T(8,128)(2,1)S(1)}, bf16[16,64,128]{2,1,0:T(8,128)(2,1)S(1)}, bf16[16,64,128]{2,1,0:T(8,128)(2,1)S(1)})) conditional(s32[]{:T(128)} %convert_element_type.35, (s32[2,2048]{1,0:T(2,128)}, bf16[16,64,128]{2,1,0:T(8,128)(2,1)}, bf16[16,64,128]{2,1,0:T(8,128)(2,1)}, ...), branch_computations={%region_4.14_spmd, %region_14.24_spmd} | conditional | flops 33759552 | bytes 9642147 | solution.py:534
  5.0 0.8 fusion.65
  6.2 0.1 compare_and_fusion.5
  6.3 0.3 convert_reduce_fusion.2
  6.7 0.1 select_reduce_fusion.7
  6.8 1.2 compare_select_fusion.6
  8.0 0.2 select_reduce_fusion.6
  8.3 0.2 fusion.30
  8.5 0.1 fusion.37
  8.7 0.2 select_reduce_fusion.5
  9.0 1.2 compare_select_fusion.7.tile_list
  10.4 0.7 select_reduce_fusion.4
  11.1 0.6 reshape.1307.send_list
  11.7 175.0 %attention.3 = (bf16[16,32,256]{2,1,0:T(8,128)(2,1)S(1)}, bf16[16,64,128]{2,1,0:T(8,128)(2,1)S(1)}, bf16[16,64,128]{2,1,0:T(8,128)(2,1)S(1)}, bf16[16,64,128]{2,1,0:T(8,128)(2,1)S(1)}) custom-call(s32[128]{0:T(128)} %reshape.1307.send_list, s32[88]{0:T(128)} %compare_select_fusion.7.tile_list, s32[16]{0:T(128)} %get-tuple-element.108.last_list, ...), custom_call_target="tpu_custom_call" | custom-call | tf_op jit(solution)/shard_map/cond/branch_1_fun/attention/pallas_call | solution.py:469
  186.7 0.7 copy.50
  187.4 0.7 copy.51
  188.1 0.7 copy.52
  188.8 0.7 copy.53
  (29 shorter events, 0.7 us)
Async XLA Ops:
  6.0 5.7 %copy-start.1 = (bf16[16,128,256]{2,1,0:T(8,128)(2,1)S(1)}, bf16[16,128,256]{2,1,0:T(8,128)(2,1)}, u32[]{:S(2)}) copy-start(bf16[16,128,256]{2,1,0:T(8,128)(2,1)} %get-tuple-element.35.og_ref) | copy-start | bytes 3145732 | tf_op jit(solution)/shard_map/cond
  6.0 5.6 %copy-start.3 = (bf16[16,64,128]{2,1,0:T(8,128)(2,1)S(1)}, bf16[16,64,128]{2,1,0:T(8,128)(2,1)}, u32[]{:S(2)}) copy-start(bf16[16,64,128]{2,1,0:T(8,128)(2,1)} %get-tuple-element.31.q_ref) | copy-start | bytes 786436 | tf_op jit(solution)/shard_map/cond
  6.0 5.6 %copy-start.5 = (bf16[16,64,128]{2,1,0:T(8,128)(2,1)S(1)}, bf16[16,64,128]{2,1,0:T(8,128)(2,1)}, u32[]{:S(2)}) copy-start(bf16[16,64,128]{2,1,0:T(8,128)(2,1)} %get-tuple-element.32.k_ref) | copy-start | bytes 786436 | tf_op jit(solution)/shard_map/cond
  6.1 5.6 %copy-start.7 = (bf16[16,64,128]{2,1,0:T(8,128)(2,1)S(1)}, bf16[16,64,128]{2,1,0:T(8,128)(2,1)}, u32[]{:S(2)}) copy-start(bf16[16,64,128]{2,1,0:T(8,128)(2,1)} %get-tuple-element.33.v_ref) | copy-start | bytes 786436 | tf_op jit(solution)/shard_map/cond
  6.1 5.6 %copy-start.9 = (bf16[64,256]{1,0:T(8,128)(2,1)S(1)}, bf16[64,256]{1,0:T(8,128)(2,1)}, u32[]{:S(2)}) copy-start(bf16[64,256]{1,0:T(8,128)(2,1)} %get-tuple-element.34.w_ref) | copy-start | bytes 98308 | tf_op jit(solution)/shard_map/cond

commit v3 on v2

v3 whole, which is shorter than its diff:
```python
import functools

import jax
import jax.numpy as jnp
from jax import lax
from jax.experimental import pallas as pl
from jax.experimental.pallas import tpu as pltpu
from jax.sharding import PartitionSpec as P

MESH = pl.DeviceIdType.MESH
HEAD = 32
NY, NZ, NX = 4, 8, 4
BLK = 16
COLUMN = 2 * NZ * BLK
UNROLL = 8
NEG = -1e30
RATE = HEAD**-0.5 * 1.4426950408889634
SCALE = HEAD**-0.5
F32 = jnp.float32
BF16 = jnp.bfloat16
VMEM_LIMIT = 61 * 2**20


def place():
    blk, hd = lax.axis_index("blk"), lax.axis_index("hd")
    core, z, y = blk % 2, (blk // 2) % NZ, blk // (2 * NZ)

    def device(yy, zz, cc, xx):
        return ((yy * NZ + zz) * 2 + cc, xx)

    return y, z, core, hd, device


def meet(peers):
    barrier = pltpu.get_barrier_semaphore()
    for peer in peers:
        pl.semaphore_signal(barrier, inc=1, device_id=peer, device_id_type=MESH)
    pl.semaphore_wait(barrier, len(peers))


class Sems:
    def __init__(self, send, recv):
        self.send, self.recv, self.used = send, recv, 0

    def take(self, count):
        self.used += count
        return self.used - count

    def copy(self, source, target, peer, sem):
        return pltpu.make_async_remote_copy(
            src_ref=source, dst_ref=target, send_sem=self.send.at[sem], recv_sem=self.recv.at[sem],
            device_id=peer, device_id_type=MESH)


class Ring:
    def __init__(self, buffer, coords, sems, pieces):
        self.buffer, self.sems, self.pieces = buffer, sems, pieces
        y, z, core, hd, device = coords
        self.z, self.core = z, core
        self.peer = (device(y, (z + 1) % NZ, core, hd), device(y, (z + NZ - 1) % NZ, core, hd))
        self.twin = device(y, z, 1 - core, hd)
        self.size = BLK // pieces
        self.leg_sem, self.twin_sem = sems.take(8 * pieces), sems.take(8 * pieces)

    def peers(self):
        return [*self.peer, self.twin]

    def rows(self, z, core, start, count):
        return self.buffer.at[pl.ds((z * 2 + core) * BLK + start, count)]

    def leg(self, piece, step, way, arriving):
        hop = step + 1 if arriving else step
        z = (self.z - hop + NZ) % NZ if way == 0 else (self.z + hop) % NZ
        start, count = piece * self.size, self.size
        if step == 3:
            count //= 2
            start += way * count
        rows = self.rows(z, self.core, start, count)
        return self.sems.copy(rows, rows, self.peer[way], self.leg_sem + (piece * 4 + step) * 2 + way)

    def pass_on(self, piece, hop, core):
        rows = self.rows((self.z + hop + NZ) % NZ, core, piece * self.size, self.size)
        return self.sems.copy(rows, rows, self.twin, self.twin_sem + piece * 8 + hop % NZ)

    def start(self):
        for piece in range(self.pieces):
            for way in (0, 1):
                self.leg(piece, 0, way, False).start()
        for piece in range(self.pieces):
            self.pass_on(piece, 0, self.core).start()

    def event(self, step, piece):
        for way in (0, 1):
            self.leg(piece, step, way, True).wait_recv()
            if step < 3:
                self.leg(piece, step + 1, way, False).start()
                self.pass_on(piece, -1 - step if way == 0 else 1 + step, self.core).start()
        if step == 3:
            self.pass_on(piece, 4, self.core).start()

    def advance(self, step):
        for piece in range(self.pieces):
            self.event(step, piece)

    def arrive(self):
        for piece in range(self.pieces):
            for hop in range(NZ):
                self.pass_on(piece, hop, 1 - self.core).wait_recv()

    def drain(self):
        for piece in range(self.pieces):
            for step in range(4):
                for way in (0, 1):
                    self.leg(piece, step, way, False).wait_send()
            for hop in range(NZ):
                self.pass_on(piece, hop, self.core).wait_send()


class Cross:
    def __init__(self, send, relay, recv, cap, coords, sems):
        self.send, self.relay, self.recv, self.cap, self.sems = send, relay, recv, cap, sems
        y, z, core, hd, device = coords
        self.peer = (device((y + 1) % NY, z, core, hd), device((y + NY - 1) % NY, z, core, hd))
        self.sem = sems.take(6)

    def peers(self):
        return [*self.peer]

    def first(self, way):
        half = self.cap // 2
        return self.sems.copy(
            self.send.at[pl.ds(self.cap + way * half, half)], self.relay.at[pl.ds(way * half, half)], self.peer[way], self.sem + way)

    def second(self, way):
        half = self.cap // 2
        return self.sems.copy(
            self.relay.at[pl.ds(way * half, half)], self.recv.at[pl.ds(2 * self.cap + way * half, half)], self.peer[way],
            self.sem + 2 + way)

    def direct(self, way):
        return self.sems.copy(
            self.send.at[pl.ds(2 * way * self.cap, self.cap)],
            self.recv.at[pl.ds((3 - 2 * way) * self.cap, self.cap)], self.peer[way], self.sem + 4 + way)

    def move(self, column, list_ref, hop, target, base):
        def body(step, carry):
            for u in range(2):
                row = step * 2 + u
                target[base + row] = column[list_ref[hop * self.cap + row]]
            return carry

        lax.fori_loop(0, self.cap // 2, body, 0)

    def pack(self, column, list_ref):
        self.move(column, list_ref, 2, self.send, self.cap)
        for way in (0, 1):
            self.first(way).start()
        self.move(column, list_ref, 1, self.send, 0)
        self.direct(0).start()
        self.move(column, list_ref, 3, self.send, 2 * self.cap)
        self.direct(1).start()
        self.move(column, list_ref, 0, self.recv, 0)

    def relay_on(self):
        for way in (0, 1):
            self.first(way).wait_recv()
            self.second(way).start()

    def arrive(self):
        for way in (0, 1):
            self.direct(way).wait_recv()
            self.second(way).wait_recv()

    def drain(self):
        for way in (0, 1):
            self.first(way).wait_send()
            self.direct(way).wait_send()
            self.second(way).wait_send()


class Spray(Cross):
    def __init__(self, send, recv, cap, coords, sems):
        self.send, self.recv, self.cap, self.sems = send, recv, cap, sems
        y, z, core, hd, device = coords
        self.peer = [device((y + hop) % NY, z, core, hd) for hop in range(1, NY)]
        self.sem = sems.take(NY - 1)

    def leg(self, hop):
        return self.sems.copy(
            self.send.at[pl.ds((hop - 1) * self.cap, self.cap)], self.recv.at[pl.ds((NY - hop) * self.cap, self.cap)],
            self.peer[hop - 1], self.sem + hop - 1)

    def pack(self, column, list_ref):
        for hop in (2, 1, 3):
            self.move(column, list_ref, hop, self.send, (hop - 1) * self.cap)
            self.leg(hop).start()
        self.move(column, list_ref, 0, self.recv, 0)

    def arrive(self):
        for hop in range(1, NY):
            self.leg(hop).wait_recv()

    def drain(self):
        for hop in range(1, NY):
            self.leg(hop).wait_send()


def spread(first, second):
    zero = jnp.zeros_like(first)
    return jnp.concatenate([jnp.concatenate([first, zero], axis=1), jnp.concatenate([zero, second], axis=1)], axis=0)


def dot(a, b):
    return jnp.dot(a, b, preferred_element_type=F32)


def dot_nt(a, b):
    return lax.dot_general(a, b, (((1,), (1,)), ((), ())), preferred_element_type=F32)


def query_tile(kv, right):
    both = dot(kv.T, right)
    scores, prob_grad = both[:, :128], both[:, 128:]
    top = jnp.max(scores, axis=0, keepdims=True)
    expo = jnp.exp2((scores - top) * RATE)
    total = jnp.sum(expo, axis=0, keepdims=True)
    weighed = jnp.sum(expo * prob_grad, axis=0, keepdims=True)
    mean = weighed / total
    change = (expo * (prob_grad - mean)).astype(BF16)
    by_expo = dot(kv, expo.astype(BF16))
    by_change = dot(kv[:HEAD], change)
    b, o = by_expo[:HEAD], by_expo[HEAD:]
    return top, total, weighed, o, by_change + mean * b, b


def query_merge(old, new, skip):
    (m0, *acc), (m1, *add) = old, new
    m1 = m1 + skip
    m = jnp.maximum(m0, m1)
    w0, w1 = jnp.exp2((m0 - m) * RATE), jnp.exp2((m1 - m) * RATE)
    return (m, *[x * w0 + y * w1 for x, y in zip(acc, add)])


def query_result(state):
    m, total, weighed, o, a, b = state
    inverse = 1.0 / total
    delta = weighed * inverse
    rows = (o * inverse).astype(BF16)
    grads = ((a - delta * b) * (inverse * SCALE)).astype(BF16)
    aux = [m + jnp.log2(total) * (1.0 / RATE), delta, jnp.zeros((6, 128), F32)]
    return jnp.concatenate([rows, grads], axis=0), jnp.concatenate(aux, axis=0)


def pack_state(state):
    return jnp.concatenate([*state[:3], jnp.zeros((5, 128), F32)], axis=0), jnp.concatenate(state[3:], axis=0)


def load_state(rows, blocks):
    return (*[rows[i:i + 1] for i in range(3)], *[blocks[HEAD * i:HEAD * i + HEAD] for i in range(3)])


def split(row):
    parts = []
    for _ in range(3):
        part = row.astype(BF16).astype(F32)
        parts.append(part)
        row = row - part
    return parts


def key_side(k, v):
    ones, none = jnp.full((3, 128), -1.0, F32), jnp.zeros((3, 128), F32)
    rest = jnp.zeros((10, 256), F32)
    minus = jnp.concatenate(
        [jnp.concatenate([ones, none], axis=1), jnp.concatenate([none, ones], axis=1), rest], axis=0).astype(BF16)
    return jnp.concatenate([spread(k, v), minus], axis=0)


def key_tile(right, qg, aux):
    both = dot(jnp.concatenate([qg, aux], axis=0).T, right)
    prob = jnp.exp2(both[:, :128] * RATE)
    change = (prob * both[:, 128:]).astype(BF16)
    return jnp.concatenate([dot(qg[:HEAD], change), dot(qg[HEAD:], prob.astype(BF16))], axis=0)


def of_head(ref, x, h):
    return ref[x, HEAD * h:HEAD * h + HEAD]


def kernel(cap, far, send_list, tile_list, last_list, count_ref, q_ref, k_ref, v_ref, w_ref, og_ref,
           out_ref, dq_ref, dk_ref, dv_ref, *scratch):
    col, recv, col_aux, recv_aux = scratch[:4], scratch[4:8], scratch[8:10], scratch[10:12]
    (send, relay, send_aux,
     right, left, self_rows, self_blocks, both_t, aux_t, aux_own, attn_own,
     outgoing, incoming, send_sem, recv_sem) = scratch[12:]
    coords = place()
    y, z, core, hd, device = coords
    own = (z * 2 + core) * BLK
    sems = Sems(send_sem, recv_sem)
    rings = [Ring(col[unit], coords, sems, 2) for unit in range(4)]
    crosses = [Cross(send.at[unit % 2], relay.at[unit], recv[unit], cap, coords, sems) for unit in range(4)]
    aux_rings = [Ring(col_aux[h], coords, sems, 1) for h in (0, 1)]
    aux_crosses = [Spray(send_aux.at[h], recv_aux[h], cap, coords, sems) for h in (0, 1)]
    partners = [device(y, z, core, (hd + hop) % NX) for hop in range(1, NX)]
    partner_sem = sems.take(NX - 1)
    count = count_ref[0]
    groups = far // UNROLL

    def each(body, low=0, high=BLK):
        def step(x, carry):
            body(x)
            return carry

        lax.fori_loop(low, high, step, 0)

    def between(groups, body, state, slots):
        number = len(slots)

        def stretch(index, state):
            for place_of, calls in enumerate(slots):
                def run_calls(calls=calls):
                    for call in calls:
                        call()

                if calls:
                    pl.when(index == place_of)(run_calls)
            return lax.fori_loop(index * groups // number, (index + 1) * groups // number, body, state)

        return lax.fori_loop(0, number, stretch, state)

    def fill_kv(x):
        for h in (0, 1):
            col[h][own + x] = jnp.concatenate([of_head(k_ref, x, h), of_head(v_ref, x, h)], axis=0)

    def fill_qg(x):
        g = dot_nt(w_ref[...], og_ref[x]).astype(BF16)
        for h in (0, 1):
            q_head, g_head = of_head(q_ref, x, h), g[HEAD * h:HEAD * h + HEAD]
            col[2 + h][own + x] = jnp.concatenate([q_head, g_head], axis=0)
            right[h, x] = spread(q_head, g_head)
            left[h, x] = key_side(of_head(k_ref, x, h), of_head(v_ref, x, h))

    def self_query(h, slots):
        def body(group, carry):
            for u in range(UNROLL):
                x = group * UNROLL + u
                state = query_tile(jnp.concatenate([of_head(k_ref, x, h), of_head(v_ref, x, h)], axis=0), right[h, x])
                self_rows[h, x], self_blocks[h, x] = pack_state(state)
                both_t[h, far + x], aux_t[h, far + x] = query_result(state)
            return carry

        between(BLK // UNROLL, body, 0, slots)

    def entry(t):
        value = tile_list[t]
        x = value // 1024
        before = tile_list[jnp.maximum(t - 1, 0)] // 1024
        return value % 1024, x, (t == 0) | (before != x)

    def far_query(h, slots):
        def body(group, state):
            tiles = []
            for u in range(UNROLL):
                row, x, _ = entry(group * UNROLL + u)
                tiles.append(query_tile(recv[h][row], right[h, x]))
            for u in range(UNROLL):
                t = group * UNROLL + u
                _, x, fresh = entry(t)
                base = load_state(self_rows[h, x], self_blocks[h, x])
                state = tuple(jnp.where(fresh, b, s) for b, s in zip(base, state))
                skip = jnp.where(t < count, 0.0, NEG).astype(F32)
                state = query_merge(state, tiles[u], skip)
                both_t[h, t], aux_t[h, t] = query_result(state)
            return state

        row, block = jnp.zeros((1, 128), F32), jnp.zeros((HEAD, 128), F32)
        between(groups, body, (row, row, row, block, block, block), slots)

    def finish_query(h):
        def body(x):
            t = last_list[x]
            stats, both = aux_t[h, t], both_t[h, t]
            aux = jnp.concatenate([*split(stats[0:1]), *split(stats[1:2]), jnp.zeros((10, 128), F32)], axis=0).astype(BF16)
            aux_own[h, x] = aux
            col_aux[h][own + x] = aux
            attn_own[x, HEAD * h:HEAD * h + HEAD] = both[:HEAD]
            dq_ref[x, HEAD * h:HEAD * h + HEAD] = both[HEAD:]

        each(body)
        aux_rings[h].start()

    def project(a):
        part = lax.dot_general(attn_own[a], w_ref[...], (((0,), (0,)), ((), ())), preferred_element_type=F32).astype(BF16)
        for x in range(NX):
            outgoing[x, a] = part[32 * x:32 * x + 32]

    def self_key(h, slots):
        def body(group, carry):
            for u in range(UNROLL):
                x = group * UNROLL + u
                terms = key_tile(left[h, x], col[2 + h][own + x], aux_own[h, x])
                self_blocks[h, x, :64] = terms
                both_t[h, far + x] = terms.astype(BF16)
            return carry

        between(BLK // UNROLL, body, 0, slots)

    def far_key(h, slots):
        def body(group, state):
            tiles = []
            for u in range(UNROLL):
                row, x, _ = entry(group * UNROLL + u)
                tiles.append(key_tile(left[h, x], recv[2 + h][row], recv_aux[h][row]))
            for u in range(UNROLL):
                t = group * UNROLL + u
                _, x, fresh = entry(t)
                use = jnp.where(t < count, 1.0, 0.0).astype(F32)
                state = jnp.where(fresh, self_blocks[h, x, :64], state) + tiles[u] * use
                both_t[h, t] = state.astype(BF16)
            return state

        between(groups, body, jnp.zeros((64, 128), F32), slots)

    def finish_key(h):
        def body(x):
            terms = both_t[h, last_list[x]]
            dk_ref[x, HEAD * h:HEAD * h + HEAD] = (terms[:HEAD].astype(F32) * SCALE).astype(BF16)
            dv_ref[x, HEAD * h:HEAD * h + HEAD] = terms[HEAD:]

        each(body)

    def land(unit):
        rings[unit].advance(3)
        rings[unit].arrive()
        crosses[unit].pack(col[unit], send_list)

    def land_aux(h):
        aux_rings[h].advance(3)
        aux_rings[h].arrive()
        aux_crosses[h].pack(col_aux[h], send_list)

    def came(cross):
        cross.arrive()
        cross.drain()

    def at(ring, step, piece=0):
        return lambda: ring.event(step, piece)

    r0, r1, r2, r3 = rings
    a0, a1 = aux_rings
    each(fill_kv)
    meet(r0.peers() + aux_crosses[0].peer + partners)
    r0.start()
    each(fill_qg)
    r0.advance(0)
    self_query(0, [[], [at(r0, 1, 0)]])
    self_query(1, [[at(r0, 1, 1)], [at(r0, 2, 0)]])
    r0.event(2, 1)
    r1.start()
    land(0)
    r1.advance(0)
    r1.event(1, 0)
    crosses[0].relay_on()
    r1.event(1, 1)
    r1.advance(2)
    r2.start()
    land(1)
    r2.event(0, 0)
    came(crosses[0])
    far_query(0, [[], [at(r2, 0, 1)], [at(r2, 1, 0), crosses[1].relay_on], [at(r2, 1, 1)]])
    finish_query(0)
    r2.event(2, 0)
    a0.event(0, 0)
    r2.event(2, 1)
    r3.start()
    a0.event(1, 0)
    land(2)
    r3.event(0, 0)
    came(crosses[1])
    far_query(1, [[at(a0, 2)], [at(r3, 0, 1)], [lambda: land_aux(0), at(r3, 1, 0)], [crosses[2].relay_on, at(r3, 1, 1)]])
    finish_query(1)
    r3.event(2, 0)
    a1.event(0, 0)
    r3.event(2, 1)
    a1.event(1, 0)
    a1.event(2, 0)
    r3.advance(3)
    land_aux(1)
    r3.arrive()
    crosses[3].pack(col[3], send_list)
    each(project)
    legs = []
    for hop in range(1, NX):
        leg = sems.copy(outgoing.at[(hd + hop) % NX], incoming.at[hop - 1], partners[hop - 1], partner_sem + hop - 1)
        leg.start()
        legs.append(leg)
    self_key(0, [[]])
    crosses[3].relay_on()
    came(crosses[2])
    came(aux_crosses[0])
    far_key(0, [[]])
    finish_key(0)
    self_key(1, [[]])
    for leg in legs:
        leg.wait()

    def total(a):
        value = outgoing[hd, a].astype(F32)
        for hop in range(NX - 1):
            value += incoming[hop, a].astype(F32)
        out_ref[a] = value.astype(BF16)

    each(total)
    came(aux_crosses[1])
    came(crosses[3])
    far_key(1, [[]])
    finish_key(1)
    for ring in rings + aux_rings:
        ring.drain()


def run(cap, far, number, send_list, tile_list, last_list, count, *arrays):
    smem = pl.BlockSpec(memory_space=pltpu.SMEM)
    vmem = pl.BlockSpec(memory_space=pltpu.VMEM)
    sem = pltpu.SemaphoreType.DMA
    half = jax.ShapeDtypeStruct((BLK, 64, 128), BF16)

    def rows(units, count):
        return pltpu.VMEM((units, count, 64, 128), BF16)

    def alone(count, height=64):
        return pltpu.VMEM((count, height, 128), BF16)

    def aux(count):
        return pltpu.VMEM((2, count, 16, 128), BF16)

    def stats(count):
        return pltpu.VMEM((2, count, 8, 128), F32)

    scratch = [
        *[alone(COLUMN)] * 4, *[alone(4 * cap)] * 4, *[alone(COLUMN, 16)] * 2, *[alone(4 * cap, 16)] * 2,
        rows(2, 3 * cap), rows(4, cap), aux(3 * cap),
        pltpu.VMEM((2, BLK, 64, 256), BF16), pltpu.VMEM((2, BLK, 80, 256), BF16),
        stats(BLK), pltpu.VMEM((2, BLK, 96, 128), F32),
        rows(2, far + BLK), stats(far + BLK),
        aux(BLK), pltpu.VMEM((BLK, 64, 128), BF16),
        pltpu.VMEM((NX, BLK, 32, 256), BF16), pltpu.VMEM((NX - 1, BLK, 32, 256), BF16),
        sem((200,)), sem((200,)),
    ]
    return pl.pallas_call(
        functools.partial(kernel, cap, far),
        out_shape=(jax.ShapeDtypeStruct((BLK, 32, 256), BF16), half, half, half),
        in_specs=[smem] * 4 + [vmem] * 5, out_specs=(vmem,) * 4, scratch_shapes=scratch,
        compiler_params=pltpu.CompilerParams(collective_id=number, has_side_effects=True, vmem_limit_bytes=VMEM_LIMIT),
        name="attention",
    )(send_list[:, :cap].reshape(-1), tile_list[:far], last_list, count, *arrays)


def before(marks):
    rows, length = marks.shape
    cut = marks.astype(BF16).reshape(rows, length // 128, 128)
    lower = (jnp.arange(128)[:, None] < jnp.arange(128)[None, :]).astype(BF16)
    inside = jnp.einsum("rsc,cd->rsd", cut, lower, preferred_element_type=F32)
    sums = jnp.sum(cut.astype(F32), axis=2)
    ahead = jnp.arange(length // 128)[:, None] < jnp.arange(length // 128)[None, :]
    starts = jnp.sum(jnp.where(ahead[None], sums[:, :, None], 0.0), axis=1)
    return (inside + starts[:, :, None]).astype(jnp.int32).reshape(rows, length), jnp.sum(sums, axis=1).astype(jnp.int32)


def lists(pair_list, cap, far):
    me = lax.axis_index("blk")
    y, rest = me // (2 * NZ), me % (2 * NZ)
    near = jnp.concatenate([pair_list[0], pair_list[1]])
    away = jnp.concatenate([pair_list[1], pair_list[0]])
    near_dev, away_col = near // BLK, away // COLUMN
    hops = jnp.arange(NY, dtype=jnp.int32)
    asked = (near_dev[None] == ((y + hops) % NY * 2 * NZ + rest)[:, None]) & (away_col == y)[None]
    mine = near_dev == me
    source = mine[None] & (away_col[None] == ((y + hops) % NY)[:, None])
    at_block = mine[None] & ((near % BLK)[None] == jnp.arange(BLK, dtype=jnp.int32)[:, None])
    rank, sums = before(jnp.concatenate([asked, source, at_block], axis=0))
    place_of = jnp.arange(cap, dtype=jnp.int32)
    hit = asked[:, None] & (rank[:NY, None] == place_of[None, :, None])
    send_list = jnp.sum(jnp.where(hit, (away % COLUMN)[None, None], 0), axis=2)
    row = jnp.sum(jnp.where(source, rank[NY:2 * NY] + hops[:, None] * cap, 0), axis=0)
    counts = sums[2 * NY:]
    starts = jnp.sum(jnp.where(jnp.arange(BLK)[None, :] < jnp.arange(BLK)[:, None], counts[None, :], 0), axis=1)
    spot = jnp.sum(jnp.where(at_block, rank[2 * NY:] + starts[:, None], 0), axis=0)
    spot = jnp.where(mine, spot, far)
    value = near % BLK * 1024 + row
    chosen = spot[None] == jnp.arange(far, dtype=jnp.int32)[:, None]
    tile_list = jnp.sum(jnp.where(chosen, value[None], 0), axis=1)
    count = jnp.sum(counts)
    tile_list = jnp.where(jnp.arange(far) < count, tile_list, (BLK - 1) * 1024)
    last_list = jnp.where(counts > 0, starts + counts - 1, far + jnp.arange(BLK))
    i32 = jnp.int32
    return send_list.astype(i32), tile_list.astype(i32), last_list.astype(i32), count[None].astype(i32)


def most(pair_list):
    near = jnp.concatenate([pair_list[0], pair_list[1]]) // BLK
    away = jnp.concatenate([pair_list[1], pair_list[0]]) // COLUMN
    bins = jnp.arange(64 * NY, dtype=jnp.int32)
    counts = jnp.sum(((near * NY + away)[None] == bins[:, None]).astype(jnp.int32), axis=1)
    return jnp.max(counts), jnp.max(jnp.sum(counts.reshape(64, NY), axis=1))


def deliver(*refs):
    copies = [pltpu.make_async_copy(refs[i], refs[4 + i], refs[8].at[i]) for i in range(4)]
    for copy in copies:
        copy.start()
    for copy in copies:
        copy.wait()


def local(queries, keys, values, out_weight, out_grad, pair_list):
    arrays = (queries, keys, values, out_weight, out_grad)

    def branch(cap, far, number):
        return lambda: run(cap, far, number, *lists(pair_list, cap, far), *arrays)

    rows, tiles = most(pair_list)
    results = lax.cond((rows <= 30) & (tiles <= 88), branch(30, 88, 0), branch(64, 160, 1))
    anywhere = pl.BlockSpec(memory_space=pl.ANY)
    return pl.pallas_call(
        deliver, out_shape=[jax.ShapeDtypeStruct(item.shape, item.dtype) for item in results],
        in_specs=[anywhere] * 4, out_specs=[anywhere] * 4, scratch_shapes=[pltpu.SemaphoreType.DMA((4,))], name="deliver")(*results)


def solution(mesh):
    blocks, weight = P("blk", "hd", None), P("hd", None)
    return jax.shard_map(
        local, mesh=mesh,
        in_specs=(blocks, blocks, blocks, weight, P("blk", None, None), P()),
        out_specs=(blocks,) * 4, check_vma=False)
```

time: 190 us -> 165 us (0.87)
  Pallas kernels: 175 us -> 152 us
  local copies, waits for them, and re-layouts: 5.28 us -> 2.56 us
    pallas_call x1, Pallas kernels: 175 us -> 151 us  [run(): pl.pallas_call(functools.partial(kernel, cap, far), out_shape=(jax.ShapeD...]
    unnamed x4 -> x0, local copies, waits for them, and re-layouts: 2.81 us -> none
where the time goes in v3:
time: 165 us; the launch traced here: 164 us
  Pallas kernels  152 us (92%)
  other arithmetic  7.05 us (4%)
  local copies, waits for them, and re-layouts  2.56 us (2%)
  between operations  2.13 us (1%)
    pallas_call x1, Pallas kernels, run(): pl.pallas_call(functools.partial(kernel, cap, far), out_shape=(jax.ShapeD...  151 us

profile of v3, /device:TPU:1, one launch (start us, length us, event | category | flops | bytes accessed | tf_op | source)
XLA Modules:
  0.0 164.1 jit_solution(16883855082275522181)
XLA Ops:
  0.6 0.8 fusion.66
  1.5 0.5 convert_reduce_fusion.4
  2.0 0.6 reduce_max.18
  3.3 0.1 reshape.1309
  3.4 0.1 reduce_sum.189
  3.5 0.6 reduce_max.19
  4.8 158.2 %conditional.1 = ((bf16[16,32,256]{2,1,0:T(8,128)(2,1)S(1)}, bf16[16,64,128]{2,1,0:T(8,128)(2,1)S(1)}, bf16[16,64,128]{2,1,0:T(8,128)(2,1)S(1)}, bf16[16,64,128]{2,1,0:T(8,128)(2,1)S(1)})) conditional(s32[]{:T(128)} %convert_element_type.35, (s32[2,2048]{1,0:T(2,128)}, bf16[16,64,128]{2,1,0:T(8,128)(2,1)}, bf16[16,64,128]{2,1,0:T(8,128)(2,1)}, ...), branch_computations={%region_4.14_spmd, %region_14.24_spmd} | conditional | flops 33759552 | bytes 9642147 | solution.py:623
  5.0 0.8 fusion.65
  6.1 0.1 compare_and_fusion.6
  6.2 0.1 compare_and_fusion.5
  6.3 0.3 convert_reduce_fusion.2
  6.7 0.1 select_reduce_fusion.7
  6.8 1.2 compare_select_fusion.6
  8.0 0.2 select_reduce_fusion.6
  8.3 0.2 fusion.30
  8.5 0.1 fusion.37
  8.7 0.2 select_reduce_fusion.5
  9.0 1.2 compare_select_fusion.7.tile_list
  10.2 0.1 compare_and_fusion.9
  10.4 1.1 select_reduce_fusion.4
  11.5 0.1 copy.10
  11.6 0.6 reshape.1307.send_list
  12.2 150.7 %attention.3 = (bf16[16,32,256]{2,1,0:T(8,128)(2,1)S(1)}, bf16[16,64,128]{2,1,0:T(8,128)(2,1)S(1)}, bf16[16,64,128]{2,1,0:T(8,128)(2,1)S(1)}, bf16[16,64,128]{2,1,0:T(8,128)(2,1)S(1)}) custom-call(s32[120]{0:T(128)} %reshape.1307.send_list, s32[88]{0:T(128)} %compare_select_fusion.7.tile_list, s32[16]{0:T(128)} %get-tuple-element.104.last_list, ...), custom_call_target="tpu_custom_call" | custom-call | tf_op jit(solution)/shard_map/cond/branch_1_fun/attention/pallas_call | solution.py:550
  162.9 1.0 deliver.1
  (27 shorter events, 0.5 us)
Async XLA Ops:
  6.0 6.1 %copy-start.1 = (bf16[16,128,256]{2,1,0:T(8,128)(2,1)S(1)}, bf16[16,128,256]{2,1,0:T(8,128)(2,1)}, u32[]{:S(2)}) copy-start(bf16[16,128,256]{2,1,0:T(8,128)(2,1)} %get-tuple-element.35.og_ref) | copy-start | bytes 3145732 | tf_op jit(solution)/shard_map/cond
  6.0 6.1 %copy-start.3 = (bf16[16,64,128]{2,1,0:T(8,128)(2,1)S(1)}, bf16[16,64,128]{2,1,0:T(8,128)(2,1)}, u32[]{:S(2)}) copy-start(bf16[16,64,128]{2,1,0:T(8,128)(2,1)} %get-tuple-element.31.q_ref) | copy-start | bytes 786436 | tf_op jit(solution)/shard_map/cond
  6.0 6.1 %copy-start.5 = (bf16[16,64,128]{2,1,0:T(8,128)(2,1)S(1)}, bf16[16,64,128]{2,1,0:T(8,128)(2,1)}, u32[]{:S(2)}) copy-start(bf16[16,64,128]{2,1,0:T(8,128)(2,1)} %get-tuple-element.32.k_ref) | copy-start | bytes 786436 | tf_op jit(solution)/shard_map/cond
  6.1 6.1 %copy-start.7 = (bf16[16,64,128]{2,1,0:T(8,128)(2,1)S(1)}, bf16[16,64,128]{2,1,0:T(8,128)(2,1)}, u32[]{:S(2)}) copy-start(bf16[16,64,128]{2,1,0:T(8,128)(2,1)} %get-tuple-element.33.v_ref) | copy-start | bytes 786436 | tf_op jit(solution)/shard_map/cond
  6.1 6.1 %copy-start.9 = (bf16[64,256]{1,0:T(8,128)(2,1)S(1)}, bf16[64,256]{1,0:T(8,128)(2,1)}, u32[]{:S(2)}) copy-start(bf16[64,256]{1,0:T(8,128)(2,1)} %get-tuple-element.34.w_ref) | copy-start | bytes 98308 | tf_op jit(solution)/shard_map/cond

commit v4 on v3

--- a/solution.py
+++ b/solution.py
@@ -53,8 +53,8 @@
 
 
 class Ring:
-    def __init__(self, buffer, coords, sems, pieces):
-        self.buffer, self.sems, self.pieces = buffer, sems, pieces
+    def __init__(self, buffer, coords, sems, pieces, height=1):
+        self.buffer, self.sems, self.pieces, self.height = buffer, sems, pieces, height
         y, z, core, hd, device = coords
         self.z, self.core = z, core
         self.peer = (device(y, (z + 1) % NZ, core, hd), device(y, (z + NZ - 1) % NZ, core, hd))
@@ -66,7 +66,7 @@
         return [*self.peer, self.twin]
 
     def rows(self, z, core, start, count):
-        return self.buffer.at[pl.ds((z * 2 + core) * BLK + start, count)]
+        return self.buffer.at[pl.ds(((z * 2 + core) * BLK + start) * self.height, count * self.height)]
 
     def leg(self, piece, step, way, arriving):
         hop = step + 1 if arriving else step
@@ -116,9 +116,14 @@
                 self.pass_on(piece, hop, self.core).wait_send()
 
 
+def stride_of(cap):
+    return (cap + 3) // 4 * 4
+
+
 class Cross:
     def __init__(self, send, relay, recv, cap, coords, sems):
         self.send, self.relay, self.recv, self.cap, self.sems = send, relay, recv, cap, sems
+        self.stride = stride_of(cap)
         y, z, core, hd, device = coords
         self.peer = (device((y + 1) % NY, z, core, hd), device((y + NY - 1) % NY, z, core, hd))
         self.sem = sems.take(6)
@@ -134,13 +139,13 @@
     def second(self, way):
         half = self.cap // 2
         return self.sems.copy(
-            self.relay.at[pl.ds(way * half, half)], self.recv.at[pl.ds(2 * self.cap + way * half, half)], self.peer[way],
+            self.relay.at[pl.ds(way * half, half)], self.recv.at[pl.ds(2 * self.stride + way * half, half)], self.peer[way],
             self.sem + 2 + way)
 
     def direct(self, way):
         return self.sems.copy(
             self.send.at[pl.ds(2 * way * self.cap, self.cap)],
-            self.recv.at[pl.ds((3 - 2 * way) * self.cap, self.cap)], self.peer[way], self.sem + 4 + way)
+            self.recv.at[pl.ds((3 - 2 * way) * self.stride, self.cap)], self.peer[way], self.sem + 4 + way)
 
     def move(self, column, list_ref, hop, target, base):
         def body(step, carry):
@@ -178,21 +183,31 @@
             self.second(way).wait_send()
 
 
-class Spray(Cross):
+class Spray:
     def __init__(self, send, recv, cap, coords, sems):
         self.send, self.recv, self.cap, self.sems = send, recv, cap, sems
+        self.rows = 2 * stride_of(cap)
         y, z, core, hd, device = coords
         self.peer = [device((y + hop) % NY, z, core, hd) for hop in range(1, NY)]
         self.sem = sems.take(NY - 1)
 
     def leg(self, hop):
         return self.sems.copy(
-            self.send.at[pl.ds((hop - 1) * self.cap, self.cap)], self.recv.at[pl.ds((NY - hop) * self.cap, self.cap)],
+            self.send.at[pl.ds((hop - 1) * self.rows, self.rows)], self.recv.at[pl.ds((NY - hop) * self.rows, self.rows)],
             self.peer[hop - 1], self.sem + hop - 1)
+
+    def move(self, column, list_ref, hop, target, base):
+        def body(step, carry):
+            for u in range(2):
+                row = step * 2 + u
+                target[pl.ds(base + 2 * row, 2)] = column[pl.ds(2 * list_ref[hop * self.cap + row], 2)]
+            return carry
+
+        lax.fori_loop(0, self.cap // 2, body, 0)
 
     def pack(self, column, list_ref):
         for hop in (2, 1, 3):
-            self.move(column, list_ref, hop, self.send, (hop - 1) * self.cap)
+            self.move(column, list_ref, hop, self.send, (hop - 1) * self.rows)
             self.leg(hop).start()
         self.move(column, list_ref, 0, self.recv, 0)
 
@@ -259,25 +274,24 @@
     return (*[rows[i:i + 1] for i in range(3)], *[blocks[HEAD * i:HEAD * i + HEAD] for i in range(3)])
 
 
-def split(row):
+def split(rows):
     parts = []
     for _ in range(3):
-        part = row.astype(BF16).astype(F32)
+        part = rows.astype(BF16).astype(F32)
         parts.append(part)
-        row = row - part
-    return parts
+        rows = rows - part
+    return jnp.concatenate([*parts, jnp.zeros((10, 128), F32)], axis=0).astype(BF16)
 
 
 def key_side(k, v):
-    ones, none = jnp.full((3, 128), -1.0, F32), jnp.zeros((3, 128), F32)
-    rest = jnp.zeros((10, 256), F32)
-    minus = jnp.concatenate(
-        [jnp.concatenate([ones, none], axis=1), jnp.concatenate([none, ones], axis=1), rest], axis=0).astype(BF16)
+    ones, none = jnp.full((1, 128), -1.0, F32), jnp.zeros((1, 128), F32)
+    pair = jnp.concatenate([jnp.concatenate([ones, none], axis=1), jnp.concatenate([none, ones], axis=1)], axis=0)
+    minus = jnp.concatenate([pair, pair, pair, jnp.zeros((10, 256), F32)], axis=0).astype(BF16)
     return jnp.concatenate([spread(k, v), minus], axis=0)
 
 
-def key_tile(right, qg, aux):
-    both = dot(jnp.concatenate([qg, aux], axis=0).T, right)
+def key_tile(right, qg, stats):
+    both = dot(jnp.concatenate([qg, split(stats)], axis=0).T, right)
     prob = jnp.exp2(both[:, :128] * RATE)
     change = (prob * both[:, 128:]).astype(BF16)
     return jnp.concatenate([dot(qg[:HEAD], change), dot(qg[HEAD:], prob.astype(BF16))], axis=0)
@@ -299,7 +313,7 @@
     sems = Sems(send_sem, recv_sem)
     rings = [Ring(col[unit], coords, sems, 2) for unit in range(4)]
     crosses = [Cross(send.at[unit % 2], relay.at[unit], recv[unit], cap, coords, sems) for unit in range(4)]
-    aux_rings = [Ring(col_aux[h], coords, sems, 1) for h in (0, 1)]
+    aux_rings = [Ring(col_aux[h], coords, sems, 1, 2) for h in (0, 1)]
     aux_crosses = [Spray(send_aux.at[h], recv_aux[h], cap, coords, sems) for h in (0, 1)]
     partners = [device(y, z, core, (hd + hop) % NX) for hop in range(1, NX)]
     partner_sem = sems.take(NX - 1)
@@ -380,9 +394,8 @@
         def body(x):
             t = last_list[x]
             stats, both = aux_t[h, t], both_t[h, t]
-            aux = jnp.concatenate([*split(stats[0:1]), *split(stats[1:2]), jnp.zeros((10, 128), F32)], axis=0).astype(BF16)
-            aux_own[h, x] = aux
-            col_aux[h][own + x] = aux
+            aux_own[h, x] = stats
+            col_aux[h][pl.ds((own + x) * 2, 2)] = stats[:2]
             attn_own[x, HEAD * h:HEAD * h + HEAD] = both[:HEAD]
             dq_ref[x, HEAD * h:HEAD * h + HEAD] = both[HEAD:]
 
@@ -398,7 +411,7 @@
         def body(group, carry):
             for u in range(UNROLL):
                 x = group * UNROLL + u
-                terms = key_tile(left[h, x], col[2 + h][own + x], aux_own[h, x])
+                terms = key_tile(left[h, x], col[2 + h][own + x], aux_own[h, x][:2])
                 self_blocks[h, x, :64] = terms
                 both_t[h, far + x] = terms.astype(BF16)
             return carry
@@ -410,7 +423,7 @@
             tiles = []
             for u in range(UNROLL):
                 row, x, _ = entry(group * UNROLL + u)
-                tiles.append(key_tile(left[h, x], recv[2 + h][row], recv_aux[h][row]))
+                tiles.append(key_tile(left[h, x], recv[2 + h][row], recv_aux[h][pl.ds(2 * row, 2)]))
             for u in range(UNROLL):
                 t = group * UNROLL + u
                 _, x, fresh = entry(t)
@@ -528,22 +541,24 @@
     def rows(units, count):
         return pltpu.VMEM((units, count, 64, 128), BF16)
 
-    def alone(count, height=64):
-        return pltpu.VMEM((count, height, 128), BF16)
-
-    def aux(count):
-        return pltpu.VMEM((2, count, 16, 128), BF16)
+    stride = stride_of(cap)
+
+    def alone(count):
+        return pltpu.VMEM((count, 64, 128), BF16)
+
+    def flat(count):
+        return pltpu.VMEM((count, 128), F32)
 
     def stats(count):
         return pltpu.VMEM((2, count, 8, 128), F32)
 
     scratch = [
-        *[alone(COLUMN)] * 4, *[alone(4 * cap)] * 4, *[alone(COLUMN, 16)] * 2, *[alone(4 * cap, 16)] * 2,
-        rows(2, 3 * cap), rows(4, cap), aux(3 * cap),
+        *[alone(COLUMN)] * 4, *[alone(4 * stride)] * 4, *[flat(2 * COLUMN)] * 2, *[flat(8 * stride)] * 2,
+        rows(2, 3 * cap), rows(4, cap), pltpu.VMEM((2, 6 * stride, 128), F32),
         pltpu.VMEM((2, BLK, 64, 256), BF16), pltpu.VMEM((2, BLK, 80, 256), BF16),
         stats(BLK), pltpu.VMEM((2, BLK, 96, 128), F32),
         rows(2, far + BLK), stats(far + BLK),
-        aux(BLK), pltpu.VMEM((BLK, 64, 128), BF16),
+        stats(BLK), pltpu.VMEM((BLK, 64, 128), BF16),
         pltpu.VMEM((NX, BLK, 32, 256), BF16), pltpu.VMEM((NX - 1, BLK, 32, 256), BF16),
         sem((200,)), sem((200,)),
     ]
@@ -553,7 +568,7 @@
         in_specs=[smem] * 4 + [vmem] * 5, out_specs=(vmem,) * 4, scratch_shapes=scratch,
         compiler_params=pltpu.CompilerParams(collective_id=number, has_side_effects=True, vmem_limit_bytes=VMEM_LIMIT),
         name="attention",
-    )(send_list[:, :cap].reshape(-1), tile_list[:far], last_list, count, *arrays)
+    )(send_list, tile_list, last_list, count, *arrays)
 
 
 def before(marks):
@@ -579,30 +594,33 @@
     source = mine[None] & (away_col[None] == ((y + hops) % NY)[:, None])
     at_block = mine[None] & ((near % BLK)[None] == jnp.arange(BLK, dtype=jnp.int32)[:, None])
     rank, sums = before(jnp.concatenate([asked, source, at_block], axis=0))
-    place_of = jnp.arange(cap, dtype=jnp.int32)
-    hit = asked[:, None] & (rank[:NY, None] == place_of[None, :, None])
-    send_list = jnp.sum(jnp.where(hit, (away % COLUMN)[None, None], 0), axis=2)
-    row = jnp.sum(jnp.where(source, rank[NY:2 * NY] + hops[:, None] * cap, 0), axis=0)
+    row = jnp.sum(jnp.where(source, rank[NY:2 * NY] + hops[:, None] * stride_of(cap), 0), axis=0)
     counts = sums[2 * NY:]
     starts = jnp.sum(jnp.where(jnp.arange(BLK)[None, :] < jnp.arange(BLK)[:, None], counts[None, :], 0), axis=1)
     spot = jnp.sum(jnp.where(at_block, rank[2 * NY:] + starts[:, None], 0), axis=0)
-    spot = jnp.where(mine, spot, far)
-    value = near % BLK * 1024 + row
-    chosen = spot[None] == jnp.arange(far, dtype=jnp.int32)[:, None]
-    tile_list = jnp.sum(jnp.where(chosen, value[None], 0), axis=1)
+    spot = jnp.where(mine, spot, -1)
+    sent_at = jnp.sum(jnp.where(asked, rank[:NY] + hops[:, None] * cap + 1, 0), axis=0) - 1
+    length = max(far, NY * cap)
+    chosen = jnp.stack([sent_at, spot])[:, None, :] == jnp.arange(length, dtype=jnp.int32)[None, :, None]
+    value = jnp.stack([away % COLUMN, near % BLK * 1024 + row])
+    both = jnp.sum(jnp.where(chosen, value[:, None, :], 0), axis=2)
     count = jnp.sum(counts)
-    tile_list = jnp.where(jnp.arange(far) < count, tile_list, (BLK - 1) * 1024)
+    send_list = both[0]
+    tile_list = jnp.where(jnp.arange(length) < count, both[1], (BLK - 1) * 1024)
     last_list = jnp.where(counts > 0, starts + counts - 1, far + jnp.arange(BLK))
     i32 = jnp.int32
     return send_list.astype(i32), tile_list.astype(i32), last_list.astype(i32), count[None].astype(i32)
 
 
-def most(pair_list):
+def fits(pair_list, cap, far):
     near = jnp.concatenate([pair_list[0], pair_list[1]]) // BLK
     away = jnp.concatenate([pair_list[1], pair_list[0]]) // COLUMN
-    bins = jnp.arange(64 * NY, dtype=jnp.int32)
-    counts = jnp.sum(((near * NY + away)[None] == bins[:, None]).astype(jnp.int32), axis=1)
-    return jnp.max(counts), jnp.max(jnp.sum(counts.reshape(64, NY), axis=1))
+    kinds = jnp.arange(NY + 1, dtype=jnp.int32)
+    devices = jnp.arange(2 * NY * NZ, dtype=jnp.int32)
+    found = (near[None, None] == devices[:, None, None]) & ((away[None, None] == kinds[None, :, None]) | (kinds == NY)[None, :, None])
+    counts = jnp.sum(found.astype(jnp.int32), axis=2)
+    limits = jnp.where(kinds == NY, far, cap)
+    return jnp.max(counts - limits[None]) <= 0
 
 
 def deliver(*refs):
@@ -619,8 +637,7 @@
     def branch(cap, far, number):
         return lambda: run(cap, far, number, *lists(pair_list, cap, far), *arrays)
 
-    rows, tiles = most(pair_list)
-    results = lax.cond((rows <= 30) & (tiles <= 88), branch(30, 88, 0), branch(64, 160, 1))
+    results = lax.cond(fits(pair_list, 30, 88), branch(30, 88, 0), branch(64, 160, 1))
     anywhere = pl.BlockSpec(memory_space=pl.ANY)
     return pl.pallas_call(
         deliver, out_shape=[jax.ShapeDtypeStruct(item.shape, item.dtype) for item in results],

time: 165 us -> 152 us (0.921)
  Pallas kernels: 152 us -> 141 us
    pallas_call x1, Pallas kernels: 151 us -> 140 us  [run(): pl.pallas_call(functools.partial(kernel, cap, far), out_shape=(jax.ShapeD...]
where the time goes in v4:
time: 152 us; the launch traced here: 151 us
  Pallas kernels  141 us (93%)
  other arithmetic  6.07 us (4%)
  local copies, waits for them, and re-layouts  2.24 us (1%)
    pallas_call x1, Pallas kernels, run(): pl.pallas_call(functools.partial(kernel, cap, far), out_shape=(jax.ShapeD...  140 us

profile of v4, /device:TPU:1, one launch (start us, length us, event | category | flops | bytes accessed | tf_op | source)
XLA Modules:
  0.0 151.1 jit_solution(12344303078778311211)
XLA Ops:
  0.7 0.8 fusion.66
  1.5 0.1 fusion.58
  1.6 0.1 iota_compare_fusion.12
  1.7 0.6 convert_reduce_fusion.4
  2.3 0.7 subtract_reduce_fusion
  3.7 146.3 %conditional.1 = ((bf16[16,32,256]{2,1,0:T(8,128)(2,1)S(1)}, bf16[16,64,128]{2,1,0:T(8,128)(2,1)S(1)}, bf16[16,64,128]{2,1,0:T(8,128)(2,1)S(1)}, bf16[16,64,128]{2,1,0:T(8,128)(2,1)S(1)})) conditional(s32[]{:T(128)} %convert_element_type.35, (s32[2,2048]{1,0:T(2,128)}, bf16[16,64,128]{2,1,0:T(8,128)(2,1)}, bf16[16,64,128]{2,1,0:T(8,128)(2,1)}, ...), branch_computations={%region_2.12_spmd, %region_12.22_spmd} | conditional | flops 33866144 | bytes 9506063 | solution.py:640
  3.9 0.8 fusion.65
  4.7 0.1 and_select_fusion.5
  5.0 0.1 compare_and_fusion.5
  5.1 0.1 compare_and_fusion.4
  5.2 0.3 convert_reduce_fusion.2
  5.5 0.1 slice.60
  5.6 0.1 select_reduce_fusion.5
  5.7 1.2 compare_select_fusion.18
  6.9 0.2 select_reduce_fusion.4
  7.2 0.2 fusion.29
  7.4 0.1 fusion.36
  7.5 0.1 fusion.43
  7.6 0.1 compare_select_fusion.12
  7.8 0.7 select_reduce_fusion.3
  8.5 1.2 compare_select_fusion.19.tile_list
  9.7 0.5 slice_bitcast_fusion.send_list
  10.3 139.7 %attention.3 = (bf16[16,32,256]{2,1,0:T(8,128)(2,1)S(1)}, bf16[16,64,128]{2,1,0:T(8,128)(2,1)S(1)}, bf16[16,64,128]{2,1,0:T(8,128)(2,1)S(1)}, bf16[16,64,128]{2,1,0:T(8,128)(2,1)S(1)}) custom-call(s32[120]{0:T(128)} %slice_bitcast_fusion.send_list, s32[120]{0:T(128)} %compare_select_fusion.19.tile_list, s32[16]{0:T(128)} %get-tuple-element.104.last_list, ...), custom_call_target="tpu_custom_call" | custom-call | tf_op jit(solution)/shard_map/cond/branch_1_fun/attention/pallas_call | solution.py:565
  149.9 1.0 deliver.1
  (26 shorter events, 0.3 us)
Async XLA Ops:
  4.8 5.4 %copy-start.1 = (bf16[16,128,256]{2,1,0:T(8,128)(2,1)S(1)}, bf16[16,128,256]{2,1,0:T(8,128)(2,1)}, u32[]{:S(2)}) copy-start(bf16[16,128,256]{2,1,0:T(8,128)(2,1)} %get-tuple-element.35.og_ref) | copy-start | bytes 3145732 | tf_op jit(solution)/shard_map/cond
  4.8 5.4 %copy-start.3 = (bf16[16,64,128]{2,1,0:T(8,128)(2,1)S(1)}, bf16[16,64,128]{2,1,0:T(8,128)(2,1)}, u32[]{:S(2)}) copy-start(bf16[16,64,128]{2,1,0:T(8,128)(2,1)} %get-tuple-element.31.q_ref) | copy-start | bytes 786436 | tf_op jit(solution)/shard_map/cond
  4.8 5.4 %copy-start.5 = (bf16[16,64,128]{2,1,0:T(8,128)(2,1)S(1)}, bf16[16,64,128]{2,1,0:T(8,128)(2,1)}, u32[]{:S(2)}) copy-start(bf16[16,64,128]{2,1,0:T(8,128)(2,1)} %get-tuple-element.32.k_ref) | copy-start | bytes 786436 | tf_op jit(solution)/shard_map/cond
  4.9 5.4 %copy-start.7 = (bf16[16,64,128]{2,1,0:T(8,128)(2,1)S(1)}, bf16[16,64,128]{2,1,0:T(8,128)(2,1)}, u32[]{:S(2)}) copy-start(bf16[16,64,128]{2,1,0:T(8,128)(2,1)} %get-tuple-element.33.v_ref) | copy-start | bytes 786436 | tf_op jit(solution)/shard_map/cond
  4.9 5.4 %copy-start.9 = (bf16[64,256]{1,0:T(8,128)(2,1)S(1)}, bf16[64,256]{1,0:T(8,128)(2,1)}, u32[]{:S(2)}) copy-start(bf16[64,256]{1,0:T(8,128)(2,1)} %get-tuple-element.34.w_ref) | copy-start | bytes 98308 | tf_op jit(solution)/shard_map/cond

commit v5 on v4

--- a/solution.py
+++ b/solution.py
@@ -301,12 +301,14 @@
     return ref[x, HEAD * h:HEAD * h + HEAD]
 
 
-def kernel(cap, far, send_list, tile_list, last_list, count_ref, q_ref, k_ref, v_ref, w_ref, og_ref,
+def kernel(cap, far, send_list, tile_list, last_list, count_ref, q_ref, k_ref, v_ref, w_ref, og_far,
            out_ref, dq_ref, dk_ref, dv_ref, *scratch):
     col, recv, col_aux, recv_aux = scratch[:4], scratch[4:8], scratch[8:10], scratch[10:12]
     (send, relay, send_aux,
      right, left, self_rows, self_blocks, both_t, aux_t, aux_own, attn_own,
-     outgoing, incoming, send_sem, recv_sem) = scratch[12:]
+     outgoing, incoming, og_ref, og_sem, send_sem, recv_sem) = scratch[12:]
+    og_copy = pltpu.make_async_copy(og_far, og_ref, og_sem)
+    og_copy.start()
     coords = place()
     y, z, core, hd, device = coords
     own = (z * 2 + core) * BLK
@@ -464,6 +466,7 @@
     each(fill_kv)
     meet(r0.peers() + aux_crosses[0].peer + partners)
     r0.start()
+    og_copy.wait()
     each(fill_qg)
     r0.advance(0)
     self_query(0, [[], [at(r0, 1, 0)]])
@@ -560,12 +563,12 @@
         rows(2, far + BLK), stats(far + BLK),
         stats(BLK), pltpu.VMEM((BLK, 64, 128), BF16),
         pltpu.VMEM((NX, BLK, 32, 256), BF16), pltpu.VMEM((NX - 1, BLK, 32, 256), BF16),
-        sem((200,)), sem((200,)),
+        pltpu.VMEM((BLK, 128, 256), BF16), sem, sem((200,)), sem((200,)),
     ]
     return pl.pallas_call(
         functools.partial(kernel, cap, far),
         out_shape=(jax.ShapeDtypeStruct((BLK, 32, 256), BF16), half, half, half),
-        in_specs=[smem] * 4 + [vmem] * 5, out_specs=(vmem,) * 4, scratch_shapes=scratch,
+        in_specs=[smem] * 4 + [vmem] * 4 + [pl.BlockSpec(memory_space=pl.ANY)], out_specs=(vmem,) * 4, scratch_shapes=scratch,
         compiler_params=pltpu.CompilerParams(collective_id=number, has_side_effects=True, vmem_limit_bytes=VMEM_LIMIT),
         name="attention",
     )(send_list, tile_list, last_list, count, *arrays)
@@ -582,11 +585,9 @@
     return (inside + starts[:, :, None]).astype(jnp.int32).reshape(rows, length), jnp.sum(sums, axis=1).astype(jnp.int32)
 
 
-def lists(pair_list, cap, far):
+def lists(near, away, cap, far):
     me = lax.axis_index("blk")
     y, rest = me // (2 * NZ), me % (2 * NZ)
-    near = jnp.concatenate([pair_list[0], pair_list[1]])
-    away = jnp.concatenate([pair_list[1], pair_list[0]])
     near_dev, away_col = near // BLK, away // COLUMN
     hops = jnp.arange(NY, dtype=jnp.int32)
     asked = (near_dev[None] == ((y + hops) % NY * 2 * NZ + rest)[:, None]) & (away_col == y)[None]
@@ -612,15 +613,13 @@
     return send_list.astype(i32), tile_list.astype(i32), last_list.astype(i32), count[None].astype(i32)
 
 
-def fits(pair_list, cap, far):
-    near = jnp.concatenate([pair_list[0], pair_list[1]]) // BLK
-    away = jnp.concatenate([pair_list[1], pair_list[0]]) // COLUMN
+def excess(near, away, cap, far):
     kinds = jnp.arange(NY + 1, dtype=jnp.int32)
     devices = jnp.arange(2 * NY * NZ, dtype=jnp.int32)
-    found = (near[None, None] == devices[:, None, None]) & ((away[None, None] == kinds[None, :, None]) | (kinds == NY)[None, :, None])
+    by_kind = (away // COLUMN == kinds[:, None]) | (kinds == NY)[:, None]
+    found = (near // BLK == devices[:, None])[:, None] & by_kind[None]
     counts = jnp.sum(found.astype(jnp.int32), axis=2)
-    limits = jnp.where(kinds == NY, far, cap)
-    return jnp.max(counts - limits[None]) <= 0
+    return jnp.max(jnp.where(kinds == NY, (counts - far) * 1000, counts - cap))
 
 
 def deliver(*refs):
@@ -632,12 +631,16 @@
 
 
 def local(queries, keys, values, out_weight, out_grad, pair_list):
+    near = jnp.concatenate([pair_list[0], pair_list[1]])
+    away = jnp.concatenate([pair_list[1], pair_list[0]])
     arrays = (queries, keys, values, out_weight, out_grad)
 
     def branch(cap, far, number):
-        return lambda: run(cap, far, number, *lists(pair_list, cap, far), *arrays)
-
-    results = lax.cond(fits(pair_list, 30, 88), branch(30, 88, 0), branch(64, 160, 1))
+        return lambda: run(cap, far, number, *lists(near, away, cap, far), *arrays)
+
+    over = excess(near, away, 28, 88)
+    index = (over > 0).astype(jnp.int32) + (over > 4).astype(jnp.int32)
+    results = lax.switch(index, [branch(28, 88, 0), branch(32, 88, 1), branch(64, 160, 2)])
     anywhere = pl.BlockSpec(memory_space=pl.ANY)
     return pl.pallas_call(
         deliver, out_shape=[jax.ShapeDtypeStruct(item.shape, item.dtype) for item in results],

time: 152 us -> 149 us (0.980)
  Pallas kernels: 141 us -> 138 us
    pallas_call x1, Pallas kernels: 140 us -> 137 us  [run(): pl.pallas_call(functools.partial(kernel, cap, far), out_shape=(jax.ShapeD...]
where the time goes in v5:
time: 149 us; the launch traced here: 148 us
  Pallas kernels  138 us (93%)
  other arithmetic  5.79 us (4%)
  between operations  2.15 us (1%)
    pallas_call x1, Pallas kernels, run(): pl.pallas_call(functools.partial(kernel, cap, far), out_shape=(jax.ShapeD...  137 us

profile of v5, /device:TPU:1, one launch (start us, length us, event | category | flops | bytes accessed | tf_op | source)
XLA Modules:
  0.0 148.3 jit_solution(8570016918578792055)
XLA Ops:
  0.6 0.8 fusion.63
  1.5 0.1 fusion.57
  1.6 0.1 iota_compare_fusion.15
  1.7 0.5 convert_reduce_fusion.6
  2.3 0.7 select_reduce_fusion.9
  4.3 142.8 %conditional.1 = ((bf16[16,32,256]{2,1,0:T(8,128)(2,1)S(1)}, bf16[16,64,128]{2,1,0:T(8,128)(2,1)S(1)}, bf16[16,64,128]{2,1,0:T(8,128)(2,1)S(1)}, bf16[16,64,128]{2,1,0:T(8,128)(2,1)S(1)})) conditional(s32[]{:T(128)} %clamp.3, (s32[4096]{0:T(1024)S(1)}, s32[4096]{0:T(1024)S(1)}, bf16[16,64,128]{2,1,0:T(8,128)(2,1)}, ...), branch_computations={%region_2.12_spmd, %region_12.22_spmd, %region_22.32_spmd} | conditional | flops 33431968 | bytes 9313579 | solution.py:643
  4.3 0.0 copy-start
  4.3 0.0 copy-start.3
  4.3 0.0 copy-start.12
  4.5 0.1 compare_and_fusion
  4.6 0.1 compare_and_fusion.1
  4.7 0.3 convert_reduce_fusion
  5.1 0.1 slice.53
  5.1 0.1 select_reduce_fusion.2
  5.2 1.2 compare_select_fusion.2
  6.5 0.2 select_reduce_fusion.1
  6.6 0.2 fusion
  6.9 0.1 fusion.8
  7.0 0.1 fusion.2
  7.2 0.6 select_reduce_fusion
  7.8 1.2 compare_select_fusion.3.tile_list
  9.1 0.5 slice_bitcast_fusion.send_list
  9.6 137.2 %attention.3 = (bf16[16,32,256]{2,1,0:T(8,128)(2,1)S(1)}, bf16[16,64,128]{2,1,0:T(8,128)(2,1)S(1)}, bf16[16,64,128]{2,1,0:T(8,128)(2,1)S(1)}, bf16[16,64,128]{2,1,0:T(8,128)(2,1)S(1)}) custom-call(s32[112]{0:T(128)} %slice_bitcast_fusion.send_list, s32[112]{0:T(128)} %compare_select_fusion.3.tile_list, s32[16]{0:T(128)} %get-tuple-element.94.last_list, ...), custom_call_target="tpu_custom_call" | custom-call | tf_op jit(solution)/shard_map/cond/branch_0_fun/attention/pallas_call | solution.py:568
  147.1 1.0 deliver.1
  (23 shorter events, 0.3 us)
Async XLA Ops:
  4.3 5.3 %copy-start = (bf16[16,128,256]{2,1,0:T(8,128)(2,1)S(1)}, bf16[16,128,256]{2,1,0:T(8,128)(2,1)}, u32[]{:S(2)}) copy-start(bf16[16,128,256]{2,1,0:T(8,128)(2,1)} %get-tuple-element.48.og_far) | copy-start | bytes 3145732 | tf_op jit(solution)/shard_map/cond
  4.3 5.3 %copy-start.3 = (bf16[16,64,128]{2,1,0:T(8,128)(2,1)S(1)}, bf16[16,64,128]{2,1,0:T(8,128)(2,1)}, u32[]{:S(2)}) copy-start(bf16[16,64,128]{2,1,0:T(8,128)(2,1)} %get-tuple-element.44.q_ref) | copy-start | bytes 786436 | tf_op jit(solution)/shard_map/cond
  4.3 5.3 %copy-start.6 = (bf16[16,64,128]{2,1,0:T(8,128)(2,1)S(1)}, bf16[16,64,128]{2,1,0:T(8,128)(2,1)}, u32[]{:S(2)}) copy-start(bf16[16,64,128]{2,1,0:T(8,128)(2,1)} %get-tuple-element.45.k_ref) | copy-start | bytes 786436 | tf_op jit(solution)/shard_map/cond
  4.3 5.3 %copy-start.9 = (bf16[16,64,128]{2,1,0:T(8,128)(2,1)S(1)}, bf16[16,64,128]{2,1,0:T(8,128)(2,1)}, u32[]{:S(2)}) copy-start(bf16[16,64,128]{2,1,0:T(8,128)(2,1)} %get-tuple-element.46.v_ref) | copy-start | bytes 786436 | tf_op jit(solution)/shard_map/cond
  4.3 5.3 %copy-start.12 = (bf16[64,256]{1,0:T(8,128)(2,1)S(1)}, bf16[64,256]{1,0:T(8,128)(2,1)}, u32[]{:S(2)}) copy-start(bf16[64,256]{1,0:T(8,128)(2,1)} %get-tuple-element.47.w_ref) | copy-start | bytes 98308 | tf_op jit(solution)/shard_map/cond

commit v6 on v5

--- a/solution.py
+++ b/solution.py
@@ -499,11 +499,11 @@
     a1.event(0, 0)
     r3.event(2, 1)
     a1.event(1, 0)
-    a1.event(2, 0)
     r3.advance(3)
-    land_aux(1)
     r3.arrive()
     crosses[3].pack(col[3], send_list)
+    a1.event(2, 0)
+    land_aux(1)
     each(project)
     legs = []
     for hop in range(1, NX):

time: 149 us -> 146 us (0.980)
  Pallas kernels: 138 us -> 135 us
    pallas_call x1, Pallas kernels: 137 us -> 134 us  [run(): pl.pallas_call(functools.partial(kernel, cap, far), out_shape=(jax.ShapeD...]
where the time goes in v6:
time: 146 us; the launch traced here: 145 us
  Pallas kernels  135 us (92%)
  other arithmetic  5.79 us (4%)
  between operations  2.15 us (1%)
    pallas_call x1, Pallas kernels, run(): pl.pallas_call(functools.partial(kernel, cap, far), out_shape=(jax.ShapeD...  134 us

profile of v6, /device:TPU:1, one launch (start us, length us, event | category | flops | bytes accessed | tf_op | source)
XLA Modules:
  0.0 145.3 jit_solution(11090596414547387729)
XLA Ops:
  0.6 0.8 fusion.63
  1.5 0.1 fusion.57
  1.6 0.1 iota_compare_fusion.15
  1.7 0.5 convert_reduce_fusion.6
  2.3 0.7 select_reduce_fusion.9
  4.3 139.8 %conditional.1 = ((bf16[16,32,256]{2,1,0:T(8,128)(2,1)S(1)}, bf16[16,64,128]{2,1,0:T(8,128)(2,1)S(1)}, bf16[16,64,128]{2,1,0:T(8,128)(2,1)S(1)}, bf16[16,64,128]{2,1,0:T(8,128)(2,1)S(1)})) conditional(s32[]{:T(128)} %clamp.3, (s32[4096]{0:T(1024)S(1)}, s32[4096]{0:T(1024)S(1)}, bf16[16,64,128]{2,1,0:T(8,128)(2,1)}, ...), branch_computations={%region_2.12_spmd, %region_12.22_spmd, %region_22.32_spmd} | conditional | flops 33431968 | bytes 9313579 | solution.py:643
  4.3 0.0 copy-start
  4.3 0.0 copy-start.9
  4.3 0.0 copy-start.12
  4.5 0.1 compare_and_fusion
  4.6 0.1 compare_and_fusion.1
  4.7 0.3 convert_reduce_fusion
  5.1 0.1 slice.53
  5.1 0.1 select_reduce_fusion.2
  5.2 1.2 compare_select_fusion.2
  6.5 0.2 select_reduce_fusion.1
  6.6 0.2 fusion
  6.9 0.1 fusion.8
  7.0 0.1 fusion.2
  7.2 0.6 select_reduce_fusion
  7.8 1.2 compare_select_fusion.3.tile_list
  9.1 0.5 slice_bitcast_fusion.send_list
  9.6 134.3 %attention.3 = (bf16[16,32,256]{2,1,0:T(8,128)(2,1)S(1)}, bf16[16,64,128]{2,1,0:T(8,128)(2,1)S(1)}, bf16[16,64,128]{2,1,0:T(8,128)(2,1)S(1)}, bf16[16,64,128]{2,1,0:T(8,128)(2,1)S(1)}) custom-call(s32[112]{0:T(128)} %slice_bitcast_fusion.send_list, s32[112]{0:T(128)} %compare_select_fusion.3.tile_list, s32[16]{0:T(128)} %get-tuple-element.94.last_list, ...), custom_call_target="tpu_custom_call" | custom-call | tf_op jit(solution)/shard_map/cond/branch_0_fun/attention/pallas_call | solution.py:568
  144.1 1.0 deliver.1
  (23 shorter events, 0.3 us)
Async XLA Ops:
  4.3 5.3 %copy-start = (bf16[16,128,256]{2,1,0:T(8,128)(2,1)S(1)}, bf16[16,128,256]{2,1,0:T(8,128)(2,1)}, u32[]{:S(2)}) copy-start(bf16[16,128,256]{2,1,0:T(8,128)(2,1)} %get-tuple-element.48.og_far) | copy-start | bytes 3145732 | tf_op jit(solution)/shard_map/cond
  4.3 5.3 %copy-start.3 = (bf16[16,64,128]{2,1,0:T(8,128)(2,1)S(1)}, bf16[16,64,128]{2,1,0:T(8,128)(2,1)}, u32[]{:S(2)}) copy-start(bf16[16,64,128]{2,1,0:T(8,128)(2,1)} %get-tuple-element.44.q_ref) | copy-start | bytes 786436 | tf_op jit(solution)/shard_map/cond
  4.3 5.3 %copy-start.6 = (bf16[16,64,128]{2,1,0:T(8,128)(2,1)S(1)}, bf16[16,64,128]{2,1,0:T(8,128)(2,1)}, u32[]{:S(2)}) copy-start(bf16[16,64,128]{2,1,0:T(8,128)(2,1)} %get-tuple-element.45.k_ref) | copy-start | bytes 786436 | tf_op jit(solution)/shard_map/cond
  4.3 5.3 %copy-start.9 = (bf16[16,64,128]{2,1,0:T(8,128)(2,1)S(1)}, bf16[16,64,128]{2,1,0:T(8,128)(2,1)}, u32[]{:S(2)}) copy-start(bf16[16,64,128]{2,1,0:T(8,128)(2,1)} %get-tuple-element.46.v_ref) | copy-start | bytes 786436 | tf_op jit(solution)/shard_map/cond
  4.3 5.3 %copy-start.12 = (bf16[64,256]{1,0:T(8,128)(2,1)S(1)}, bf16[64,256]{1,0:T(8,128)(2,1)}, u32[]{:S(2)}) copy-start(bf16[64,256]{1,0:T(8,128)(2,1)} %get-tuple-element.47.w_ref) | copy-start | bytes 98308 | tf_op jit(solution)/shard_map/cond
